TPU v7x, 32 devices: a whole 2x2x4 slice. The times are simulated.
32 devices in a mesh: gz: 8 (over y, x, core), gy: 4 (over z).
Axes of the slice: x: 2, y: 2, z: 4, core: 2. Of those that a mesh axis runs over, the one named last changes fastest.
Arguments:
- applied_load: float32 [3, 64, 32, 512], P(None, 'gz', 'gy'), may hold values from -12 to 12
- start_field: float32 [3, 64, 32, 512], P(None, 'gz', 'gy'), may hold values from -2 to 2
- bone_mask: int32 [64, 32, 512], P('gz', 'gy'), may hold values 0 or 1
- element_stiffness: bfloat16 [24, 24], replicated, may hold values from -1.5 to 2, as said below
Outputs:
- corrected: float32 [3, 64, 32, 512], P(None, 'gz', 'gy')
Inputs may be any that keep to these rules, and one draw needn't show every extreme that they name: element_stiffness is symmetric and positive definite, and each of its diagonal entries is at least 0.125.
All inputs are finite; a program needn't handle non-finite values. No bound on the sum of `bone_mask` on one device may be relied on, other than what follows from the above.
Results may differ from a plain program's by a relative error of at most 0.0059.
Values may be sent and summed in bfloat16 or wider, within the bound.
A program may use at most 64 MiB of HBM per device.

v0:
```python
import functools

import jax
import jax.numpy as jnp
import ml_dtypes
import numpy as np
from jax import lax
from jax.experimental import pallas as pl
from jax.experimental.pallas import tpu as pltpu
from jax.sharding import PartitionSpec as P

DOF = 3
EDOF = 24
B = 8
C = B // 2
LOW = 0.1
MESH = pl.DeviceIdType.MESH
F32, BF16 = jnp.float32, jnp.bfloat16

NEAR = [(0, -1), (0, 1), (-1, -1), (-1, 1), (1, -1), (1, 1), (-1, 0), (1, 0)]
SPAN = [(0, 32), (32, 32), (64, 16), (80, 16), (96, 16), (112, 16), (128, 32), (160, 32)]
MASK_SPAN = {(-1, 0): 64, (0, -1): 80, (-1, -1): 96}


def col_code(col):
    p, rest = divmod(col, 64)
    sx, rc = divmod(rest, 32)
    if rc < 24:
        return p, sx, rc // 8, rc % 8
    if rc < 27:
        return p, sx, rc - 24, -1
    if rc < 30:
        return p, sx, rc - 27, 8
    return None


def tables(nx):
    half = nx // 2
    out = {}
    rep = np.zeros((192, EDOF))
    for r in range(192):
        rep[r, (r // 24) * 3 + (r % 24) // 8] = 1
    out["rep"] = rep
    rep_x = np.zeros((64, EDOF))
    for q in range(8):
        for d in range(3):
            rep_x[q * 8 + d, q * 3 + d] = 1
    out["rep_x"] = rep_x
    for cz2 in range(2):
        for cy2 in range(2):
            pick = np.zeros((32, 192))
            keep = np.zeros((192, 192))
            for col in range(192):
                code = col_code(col)
                if code is None:
                    continue
                p, sx, d, y2 = code
                pick[3 * (4 * cz2 + 2 * cy2 + sx) + d, col] = 1
                for r in range(192):
                    q, y = r // 24, r % 8
                    cz, cy = q // 4, (q // 2) % 2
                    if p == 1 - cz + cz2 and y2 == y - cy + cy2:
                        keep[r, col] = 1
            out["pick%d%d" % (cz2, cy2)] = pick
            out["keep%d%d" % (cz2, cy2)] = keep
    sel = np.zeros((128, 192))
    for z in range(B):
        for d in range(3):
            sel[z * 3 + d, z * 24 + d * 8] = 1
            sel[32 + z * 3 + d, z * 24 + d * 8 + 7] = 1
    for k, (z, y) in enumerate([(0, 0), (0, 7), (7, 0), (7, 7)]):
        for d in range(3):
            sel[64 + 16 * k + d, z * 24 + d * 8 + y] = 1
    out["sel"] = sel
    put = np.zeros((80, 128))
    for d in range(3):
        for z in range(B):
            put[(z + 1) * 8 + d, z * 3 + d] = 1
            put[(z + 1) * 8 + 3 + d, 32 + z * 3 + d] = 1
        put[d, 64 + d] = 1
        put[3 + d, 80 + d] = 1
        put[72 + d, 96 + d] = 1
        put[72 + 3 + d, 112 + d] = 1
    out["put"] = put
    mask_sel = np.zeros((64, 64))
    for i in range(8):
        mask_sel[i, 56 + i] = 1
        mask_sel[16 + i, i * 8 + 7] = 1
    mask_sel[32, 63] = 1
    for z in range(B):
        for y in range(B):
            mask_sel[48 + (z // 2) * C + y // 2, z * 8 + y] = 0.25
    out["mask_sel"] = mask_sel
    mask_put = np.zeros((144, 112))
    for layer in range(-1, B):
        for y in range(B):
            for cy in range(2):
                row, y2 = (layer + 1) * 16 + cy * 8 + y, y - cy
                if layer >= 0:
                    mask_put[row, layer * 8 + y2 if y2 >= 0 else 80 + layer] = 1
                else:
                    mask_put[row, 64 + y2 if y2 >= 0 else 96] = 1
    out["mask_put"] = mask_put
    pairs = np.zeros((nx, half))
    down = np.zeros((nx, half))
    for i in range(nx):
        pairs[i, i // 2] = 1
        if i % 2 == 0:
            down[i, i // 2] = 1
        else:
            down[i, i // 2] = 0.5
            if i // 2 + 1 < half:
                down[i, i // 2 + 1] = 0.5
    out["pairs"], out["down"] = pairs, down
    up = down.T
    out["up0"], out["up1"] = up[:, :half], up[:, half:]
    cs_put = np.zeros((320, 144))

    def place(index):
        return (index + C) // C, (index + C) % C

    for layer in range(-3, 7):
        zs, kz = place(layer)
        base = (layer + 3) * 32
        for t in range(8):
            for cy in range(2):
                ys, ky = place(t - 1 - cy)
                cs_put[base + cy * 8 + t, (zs * 3 + ys) * 16 + kz * C + ky] = 1
        for d in range(3):
            for cy in range(2):
                ys, ky = place(-2 - cy)
                cs_put[base + 16 + cy * 8 + d, (zs * 3 + ys) * 16 + kz * C + ky] = 1
    out["cs_put"] = cs_put
    line = np.zeros((C + 1, B))
    for i in range(B):
        if i % 2 == 0:
            line[i // 2, i] = 1
        else:
            line[i // 2, i] = 0.5
            line[i // 2 + 1, i] = 0.5
    shrink = np.zeros((80, 192))
    grow = np.zeros((192, 120))
    for k in range(C + 1):
        for j in range(C + 1):
            for z in range(B):
                for y in range(B):
                    for d in range(3):
                        w = line[k, z] * line[j, y]
                        shrink[k * 16 + j * 3 + d, z * 24 + d * 8 + y] = w
                        grow[z * 24 + d * 8 + y, k * 24 + d * 8 + j + 1] = w
    out["shrink"], out["grow"] = shrink, grow
    gather = np.zeros((32, 64))
    for d in range(3):
        for t in range(8):
            y = t - 1
            for slot, at in ((0, y + C), (1, y), (2, y - C), (3, y)):
                if 0 <= at <= C:
                    gather[d * 8 + t, slot * 16 + at * 3 + d] = 1
        gather[24 + d, (C - 2) * 3 + d] = 1
    out["gather"] = gather
    return out


def pack_tables(nx):
    width = max(256, nx // 2)
    where, parts, at = {}, [], 0
    for name, table in tables(nx).items():
        rows, cols = table.shape
        where[name] = (at, rows, cols)
        tall = -(-rows // 16) * 16
        padded = np.zeros((tall, width), np.float32)
        padded[:rows, :cols] = table
        parts.append(padded)
        at += tall
    return where, np.concatenate(parts).astype(ml_dtypes.bfloat16)


def kernel(where, n_z, n_y, load, start, mask, stiff, tab, out, xs, upd, inv, idle, ss, vb, sb, rb, mr, ms, cs, cr, rs, cx, cu, cinv, cidle, css, crhs, cvb,
           wmat, send_sem, recv_sem, msend, mrecv, csend, crecv, rsend, rrecv):
    nx = load.shape[-1]
    half = nx // 2
    gz, gy = lax.axis_index("gz"), lax.axis_index("gy")

    def t(name, rows=None):
        at, r, c = where[name]
        return tab[at : at + (rows or r), :c]

    def dot(a, b):
        return jnp.dot(a, b, preferred_element_type=F32)

    def exists(dz, dy):
        ok = None
        for delta, pos, n in ((dz, gz, n_z), (dy, gy, n_y)):
            if delta:
                test = pos > 0 if delta < 0 else pos < n - 1
                ok = test if ok is None else jnp.logical_and(ok, test)
        return ok

    barrier = pltpu.get_barrier_semaphore()
    count = 0
    for dz, dy in NEAR:
        ok = exists(dz, dy)
        count = count + ok.astype(jnp.int32)

        @pl.when(ok)
        def _():
            pl.semaphore_signal(barrier, inc=1, device_id=(gz + dz, gy + dy), device_id_type=MESH)

    for k, (dz, dy) in enumerate(NEAR):
        at, size = SPAN[k]

        @pl.when(jnp.logical_not(exists(dz, dy)))
        def _():
            for p in range(4):
                rb[p, at : at + size] = jnp.zeros((size, nx), BF16)
            slot = ((dz + 1) * 3 + dy + 1) * 16
            cr[slot : slot + 16] = jnp.zeros((16, half), BF16)
            if (dz, dy) in MASK_SPAN:
                m = MASK_SPAN[dz, dy]
                mr[m : m + 16] = jnp.zeros((16, nx), BF16)
            rs[dz + 1, :, (dy + 1) * 16 : (dy + 2) * 16] = jnp.zeros((5, 16, half), BF16)

    def field_copy(p, k):
        dz, dy = NEAR[k]
        back = NEAR.index((-dz, -dy))
        at, size = SPAN[k]
        to = SPAN[back][0]
        return pltpu.make_async_remote_copy(
            src_ref=sb.at[p, at : at + size], dst_ref=rb.at[p, to : to + size],
            send_sem=send_sem.at[p, k], recv_sem=recv_sem.at[p, back],
            device_id=(gz + dz, gy + dy), device_id_type=MESH)

    def field_arrival(p, k):
        at, size = SPAN[k]
        return pltpu.make_async_remote_copy(
            src_ref=sb.at[p, at : at + size], dst_ref=rb.at[p, at : at + size],
            send_sem=send_sem.at[p, k], recv_sem=recv_sem.at[p, k],
            device_id=(gz, gy), device_id_type=MESH)

    def mask_copy(k, dz, dy):
        at = 16 * k
        to = MASK_SPAN[-dz, -dy]
        return pltpu.make_async_remote_copy(
            src_ref=ms.at[at : at + 16], dst_ref=mr.at[to : to + 16],
            send_sem=msend.at[k], recv_sem=mrecv.at[k],
            device_id=(gz + dz, gy + dy), device_id_type=MESH)

    def scale_copy(k):
        dz, dy = NEAR[k]
        to = ((1 - dz) * 3 + 1 - dy) * 16
        return pltpu.make_async_remote_copy(
            src_ref=cs.at[...], dst_ref=cr.at[to : to + 16],
            send_sem=csend.at[k], recv_sem=crecv.at[NEAR.index((-dz, -dy))],
            device_id=(gz + dz, gy + dy), device_id_type=MESH)

    def rhs_part(dz):
        return (0, 5) if dz == 0 else ((0, 3) if dz < 0 else (2, 3))

    def rhs_copy(k):
        dz, dy = NEAR[k]
        first, n = rhs_part(dz)
        to = (1 - dy) * 16
        return pltpu.make_async_remote_copy(
            src_ref=rs.at[1, first : first + n, 16:32], dst_ref=rs.at[1 - dz, first : first + n, to : to + 16],
            send_sem=rsend.at[k], recv_sem=rrecv.at[NEAR.index((-dz, -dy))],
            device_id=(gz + dz, gy + dy), device_id_type=MESH)

    mask_to = [(1, 0), (0, 1), (1, 1)]

    def pack_field(p, planes):
        own = jnp.concatenate(planes, axis=0).astype(BF16)
        sb[p, 0:128] = dot(t("sel"), own).astype(BF16)
        zero = jnp.zeros((8, nx), F32)
        sb[p, 128:160] = jnp.concatenate(planes[0:3] + [zero], axis=0).astype(BF16)
        sb[p, 160:192] = jnp.concatenate(planes[21:24] + [zero], axis=0).astype(BF16)

    def send_field(p):
        for k, (dz, dy) in enumerate(NEAR):

            @pl.when(exists(dz, dy))
            def _():
                field_copy(p, k).start()

    def await_field(p):
        for k, (dz, dy) in enumerate(NEAR):

            @pl.when(exists(dz, dy))
            def _():
                field_arrival(p, k).wait_recv()

    pack_field(0, [start[d, z] for z in range(B) for d in range(3)])
    mask_own = jnp.concatenate([mask[z] for z in range(B)], axis=0).astype(F32).astype(BF16)
    mr[0:64] = mask_own
    picked = dot(t("mask_sel"), mask_own).astype(BF16)
    ms[...] = picked[0:48]
    cs[...] = dot(picked[48:64], t("pairs")).astype(BF16)
    cr[64:80] = cs[...]

    pl.semaphore_wait(barrier, count)
    send_field(0)
    for k, (dz, dy) in enumerate(mask_to):

        @pl.when(exists(dz, dy))
        def _():
            mask_copy(k, dz, dy).start()

    for k, (dz, dy) in enumerate(NEAR):

        @pl.when(exists(dz, dy))
        def _():
            scale_copy(k).start()

    stiff_bf = stiff[...]
    stiff_wide = stiff_bf.astype(F32)
    eye = lax.broadcasted_iota(jnp.int32, (EDOF, EDOF), 0) == lax.broadcasted_iota(jnp.int32, (EDOF, EDOF), 1)
    diag_mat = jnp.where(eye, stiff_wide, 0.0)
    bound = jnp.max(jnp.sum(jnp.abs(stiff_wide), axis=1, keepdims=True) / jnp.sum(diag_mat, axis=1, keepdims=True), axis=0, keepdims=True)
    rows_of = dot(t("rep"), stiff_bf).astype(BF16)
    total = None
    for cz2 in range(2):
        for cy2 in range(2):
            name = "%d%d" % (cz2, cy2)
            term = dot(rows_of, t("pick" + name, EDOF)) * t("keep" + name).astype(F32)
            total = term if total is None else total + term
    wmat[...] = total.astype(BF16)
    diag_bf = diag_mat.astype(BF16)
    diag_col = jnp.sum(dot(t("rep"), diag_bf), axis=1, keepdims=True)
    diag_col_x = jnp.sum(dot(t("rep_x"), diag_bf), axis=1, keepdims=True)

    def shift_up(v):
        lane = lax.broadcasted_iota(jnp.int32, v.shape, 1)
        return jnp.where(lane == 0, 0.0, pltpu.roll(v, 1, axis=1))

    def shift_down(v):
        n = v.shape[1]
        lane = lax.broadcasted_iota(jnp.int32, v.shape, 1)
        return jnp.where(lane == n - 1, 0.0, pltpu.roll(v, n - 1, axis=1))

    def diagonal(scale, z, d):
        sums = []
        for c in range(2):
            s = None
            for cz in range(2):
                for cy in range(2):
                    at = (4 * cz + 2 * cy + c) * 24 + d * 8
                    term = diag_col[at : at + 8] * scale(z - cz, cy)
                    s = term if s is None else s + term
            sums.append(s)
        return sums[0] + shift_up(sums[1])

    def apply(planes, scale_now, scale_below):
        terms = dot(wmat[...], planes)
        sums = []
        for c in range(2):
            parts = []
            for d in range(3):
                s = None
                for cz, sc in ((0, scale_now), (1, scale_below)):
                    for cy in range(2):
                        at = (4 * cz + 2 * cy + c) * 24 + d * 8
                        term = terms[at : at + 8] * sc[cy * 8 : cy * 8 + 8]
                        s = term if s is None else s + term
                parts.append(s)
            sums.append(jnp.concatenate(parts, axis=0))
        return sums[0] + shift_up(sums[1])

    def put_plane(ref, z, rows):
        ref[z, 0:32] = rows.astype(BF16)
        ref[z, 32:64] = shift_down(rows).astype(BF16)

    def build(p, x_of):
        placed = dot(t("put"), rb[p, 0:128])
        for z in range(B):
            put_plane(vb, z + 1, jnp.concatenate([x_of(z, d) for d in range(3)] + [placed[8 * z + 8 : 8 * z + 16]], axis=0))
        for z, at in ((0, 128), (B + 1, 160)):
            put_plane(vb, z, jnp.concatenate([rb[p, at : at + 32].astype(F32)[0:24], placed[8 * z : 8 * z + 8]], axis=0))

    for k, (dz, dy) in enumerate(mask_to):

        @pl.when(exists(-dz, -dy))
        def _():
            mask_copy(k, dz, dy).wait_recv()

    ss[...] = dot(t("mask_put"), mr[...]).reshape(B + 1, 16, nx)

    def prepare(z, carry):
        for d in range(3):
            dg = diagonal(lambda layer, cy: ss[layer + 1, cy * 8 : cy * 8 + 8], z, d)
            no = jnp.where(dg == 0.0, 1.0, 0.0)
            inv[z, d * 8 : d * 8 + 8] = 1.0 / ((dg + no) * bound)
            if d == 0:
                idle[z] = no
        return carry

    lax.fori_loop(0, B, prepare, 0)

    ratio = (1.0 + LOW) / (1.0 - LOW)
    rho = [1.0 / ratio]
    for _ in range(2):
        rho.append(1.0 / (2.0 * ratio - rho[-1]))
    steps = [(0.0, 1.0 / (0.5 * (1.0 + LOW)))]
    for i in range(2):
        steps.append((rho[i + 1] * rho[i], 2.0 * rho[i + 1] / (0.5 * (1.0 - LOW))))

    def stack(ref, z):
        return jnp.concatenate([ref[0, z], ref[1, z], ref[2, z]], axis=0)

    def three(v):
        return jnp.concatenate([v, v, v], axis=0)

    for p in range(4):
        if p > 0:
            pack_field(p, [xs[z, 8 * d : 8 * d + 8] for z in range(B) for d in range(3)])
            send_field(p)
        await_field(p)
        if p == 0:
            build(p, lambda z, d: start[d, z])
        else:
            build(p, lambda z, d: xs[z, 8 * d : 8 * d + 8])

        def plane(z):
            x = stack(start, z) if p == 0 else xs[z]
            kv = apply(vb[pl.ds(z, 3)].reshape(192, nx), ss[z + 1], ss[z])
            r = stack(load, z) - kv - three(idle[z]) * x
            if p < 3:
                u = steps[p][1] * inv[z] * r
                if p > 0:
                    u = u + steps[p][0] * upd[z]
                xs[z] = x + u
                upd[z] = u
            else:
                upd[z] = r

        def two(i, carry):
            for j in range(4):
                plane(4 * i + j)
            return carry

        lax.fori_loop(0, B // 4, two, 0)

    def split(v):
        hi = v.astype(BF16)
        return hi, (v - hi.astype(F32)).astype(BF16)

    hi, lo = split(upd[...].reshape(192, nx))
    narrow = dot(t("shrink"), hi) + dot(t("shrink"), lo)
    hi, lo = split(narrow)
    partial = dot(hi, t("down")) + dot(lo, t("down"))
    hi, lo = split(partial)
    rs[1, :, 16:32] = hi.reshape(5, 16, half)
    rs[1, :, 48:64] = lo.reshape(5, 16, half)
    for k, (dz, dy) in enumerate(NEAR):

        @pl.when(exists(dz, dy))
        def _():
            rhs_copy(k).start()

    for k, (dz, dy) in enumerate(NEAR):

        @pl.when(exists(dz, dy))
        def _():
            scale_copy(NEAR.index((-dz, -dy))).wait_recv()

    css[...] = dot(t("cs_put"), cr[...]).reshape(10, 32, half)
    last_z, last_y = gz == n_z - 1, gy == n_y - 1
    row8 = lax.broadcasted_iota(jnp.int32, (8, half), 0)
    good_y = jnp.where(jnp.logical_and(last_y, row8 >= C + 1), 0.0, 1.0)
    for k in range(9):
        good = good_y
        if k - 2 >= C:
            good = good * jnp.where(last_z, 0.0, 1.0)
        for d in range(3):
            dg = diagonal(lambda layer, cy: css[layer + 1, cy * 8 : cy * 8 + 8], k, d)
            no = jnp.where(dg == 0.0, 1.0, 0.0)
            cinv[k, d * 8 : d * 8 + 8] = good / ((dg + no) * bound)
            if d == 0:
                cidle[k] = no
        sums = []
        for c in range(2):
            s = None
            for cz in range(2):
                for cy in range(2):
                    at = (4 * cz + 2 * cy + c) * 8
                    term = diag_col_x[at : at + 8] * css[k + 1 - cz, 16 + cy * 8 : 24 + cy * 8]
                    s = term if s is None else s + term
            sums.append(s)
        dg = sums[0] + shift_up(sums[1])
        no = jnp.where(dg == 0.0, 1.0, 0.0)
        extra = 1.0 / ((dg + no) * bound)
        if k - 2 >= C:
            extra = extra * jnp.where(last_z, 0.0, 1.0)
        cinv[k, 24:32] = extra

    for k, (dz, dy) in enumerate(NEAR):

        @pl.when(exists(dz, dy))
        def _():
            rhs_copy(NEAR.index((-dz, -dy))).wait_recv()

    for k in range(9):
        kz = k - 2
        total = None
        for zs, at in ((0, kz + C), (1, kz), (2, kz - C)):
            if 0 <= at <= C:
                rows = 64 if zs == 1 else 48
                where_at = where["gather"][0]
                term = dot(tab[where_at : where_at + 32, :rows], rs[zs, at, 0:rows])
                total = term if total is None else total + term
        crhs[k] = total[0:24]
        x = steps[0][1] * cinv[k] * total
        cx[k] = x[0:24]
        cu[k] = x[0:24]
        put_plane(cvb, k, x)

    zero8 = jnp.zeros((8, half), F32)
    for p, (first, last) in ((1, (1, 7)), (2, (2, 6))):
        for k in range(first, last + 1):
            kv = apply(cvb[k - 1 : k + 2].reshape(192, half), css[k + 1], css[k])
            x = cx[k]
            r = crhs[k] - kv - three(cidle[k]) * x
            u = steps[p][0] * cu[k] + steps[p][1] * cinv[k, 0:24] * r
            cx[k] = x + u
            cu[k] = u
        if p == 1:
            for k in range(first, last + 1):
                put_plane(cvb, k, jnp.concatenate([cx[k], zero8], axis=0))

    fix = cx[2:7].reshape(120, half).astype(BF16)
    hi, lo = split(dot(t("grow"), fix))
    for c in range(2):
        side = dot(hi, t("up%d" % c)) + dot(lo, t("up%d" % c))
        lanes = slice(c * half, (c + 1) * half)
        for z in range(B):
            for d in range(3):
                at = z * 24 + d * 8
                out[d, z, :, lanes] = xs[z, 8 * d : 8 * d + 8, lanes] + side[at : at + 8]

    for k, (dz, dy) in enumerate(NEAR):

        @pl.when(exists(dz, dy))
        def _():
            for p in range(4):
                field_copy(p, k).wait_send()
            scale_copy(k).wait_send()
            rhs_copy(k).wait_send()

    for k, (dz, dy) in enumerate(mask_to):

        @pl.when(exists(dz, dy))
        def _():
            mask_copy(k, dz, dy).wait_send()


def body(n_z, n_y, load, start, mask, stiff):
    nx = load.shape[-1]
    half = nx // 2
    where, packed = pack_tables(nx)
    dma = pltpu.SemaphoreType.DMA
    vmem = pl.BlockSpec(memory_space=pltpu.VMEM)
    return pl.pallas_call(
        functools.partial(kernel, where, n_z, n_y),
        out_shape=jax.ShapeDtypeStruct(load.shape, F32),
        in_specs=[vmem] * 5,
        out_specs=vmem,
        scratch_shapes=[
            pltpu.VMEM((B, 24, nx), F32),
            pltpu.VMEM((B, 24, nx), F32),
            pltpu.VMEM((B, 24, nx), F32),
            pltpu.VMEM((B, 8, nx), F32),
            pltpu.VMEM((B + 1, 16, nx), F32),
            pltpu.VMEM((B + 2, 64, nx), BF16),
            pltpu.VMEM((4, 192, nx), BF16),
            pltpu.VMEM((4, 192, nx), BF16),
            pltpu.VMEM((112, nx), BF16),
            pltpu.VMEM((48, nx), BF16),
            pltpu.VMEM((16, half), BF16),
            pltpu.VMEM((144, half), BF16),
            pltpu.VMEM((3, 5, 64, half), BF16),
            pltpu.VMEM((9, 24, half), F32),
            pltpu.VMEM((9, 24, half), F32),
            pltpu.VMEM((9, 32, half), F32),
            pltpu.VMEM((9, 8, half), F32),
            pltpu.VMEM((10, 32, half), F32),
            pltpu.VMEM((9, 24, half), F32),
            pltpu.VMEM((9, 64, half), BF16),
            pltpu.VMEM((192, 192), BF16),
            dma((4, 8)), dma((4, 8)), dma((3,)), dma((3,)), dma((8,)), dma((8,)), dma((8,)), dma((8,)),
        ],
        compiler_params=pltpu.CompilerParams(collective_id=0, has_side_effects=True, vmem_limit_bytes=48 * 1024 * 1024),
    )(load, start, mask, stiff, jnp.asarray(packed))


def solution(mesh):
    in_specs = (P(None, "gz", "gy", None), P(None, "gz", "gy", None), P("gz", "gy", None), P())
    out_specs = P(None, "gz", "gy", None)
    fn = functools.partial(body, mesh.shape["gz"], mesh.shape["gy"])
    return jax.shard_map(fn, mesh=mesh, in_specs=in_specs, out_specs=out_specs, check_vma=False)
```

profile of v0, /device:TPU:3, one launch (start us, length us, event | category | flops | bytes accessed | tf_op | source)
XLA Modules:
  0.0 38.3 jit_solution(6228987238898404478)
XLA Ops:
  0.0 0.0 copy-start
  0.0 1.5 %copy-done = bf16[3728,256]{1,0:T(8,128)(2,1)S(1)} copy-done((bf16[3728,256]{1,0:T(8,128)(2,1)S(1)}, bf16[3728,256]{1,0:T(8,128)(2,1)}, u32[]{:S(2)}) %copy-start) | copy-done | bytes 1908760
  1.5 0.0 copy-start.1
  1.5 1.0 %copy-done.1 = f32[3,8,8,512]{3,2,1,0:T(8,128)S(1)} copy-done((f32[3,8,8,512]{3,2,1,0:T(8,128)S(1)}, f32[3,8,8,512]{3,2,1,0:T(8,128)}, u32[]{:S(2)}) %copy-start.1) | copy-done | bytes 393240
  2.5 0.0 copy-start.2
  2.5 1.0 %copy-done.2 = f32[3,8,8,512]{3,2,1,0:T(8,128)S(1)} copy-done((f32[3,8,8,512]{3,2,1,0:T(8,128)S(1)}, f32[3,8,8,512]{3,2,1,0:T(8,128)}, u32[]{:S(2)}) %copy-start.2) | copy-done | bytes 393240
  3.5 0.0 copy-start.3
  3.5 0.9 %copy-done.3 = s32[8,8,512]{2,1,0:T(8,128)S(1)} copy-done((s32[8,8,512]{2,1,0:T(8,128)S(1)}, s32[8,8,512]{2,1,0:T(8,128)}, u32[]{:S(2)}) %copy-start.3) | copy-done | bytes 131096
  4.4 0.0 copy-start.4
  4.4 0.7 %copy-done.4 = bf16[24,24]{1,0:T(8,128)(2,1)S(1)} copy-done((bf16[24,24]{1,0:T(8,128)(2,1)S(1)}, bf16[24,24]{1,0:T(8,128)(2,1)}, u32[]{:S(2)}) %copy-start.4) | copy-done | bytes 1176
  5.1 32.4 %shard_map.55 = f32[3,8,8,512]{3,2,1,0:T(8,128)S(1)} custom-call(f32[3,8,8,512]{3,2,1,0:T(8,128)S(1)} %copy-done.1, f32[3,8,8,512]{3,2,1,0:T(8,128)S(1)} %copy-done.2, s32[8,8,512]{2,1,0:T(8,128)S(1)} %copy-done.3, bf16[24,24]{1,0:T(8,128)(2,1)S(1)} %copy-done.4, bf16[3728,256]{1,0:T(8,128)(2,1)S(1)} %copy-done), custom_call_target="tpu_custom_call" | custom-call | tf_op jit(solution)/shard_map/pallas_call | solution.py:560
  37.5 0.7 %copy.7 = f32[3,8,8,512]{3,2,1,0:T(8,128)} copy(f32[3,8,8,512]{3,2,1,0:T(8,128)S(1)} %shard_map.55) | data formatting | bytes 786432
Async XLA Ops:
  0.0 1.5 %copy-start = (bf16[3728,256]{1,0:T(8,128)(2,1)S(1)}, bf16[3728,256]{1,0:T(8,128)(2,1)}, u32[]{:S(2)}) copy-start(bf16[3728,256]{1,0:T(8,128)(2,1)} %constant.2.clone.tab) | copy-start | bytes 5726212
  1.5 1.0 %copy-start.1 = (f32[3,8,8,512]{3,2,1,0:T(8,128)S(1)}, f32[3,8,8,512]{3,2,1,0:T(8,128)}, u32[]{:S(2)}) copy-start(f32[3,8,8,512]{3,2,1,0:T(8,128)} %load.1) | copy-start | bytes 1179652
  2.5 1.0 %copy-start.2 = (f32[3,8,8,512]{3,2,1,0:T(8,128)S(1)}, f32[3,8,8,512]{3,2,1,0:T(8,128)}, u32[]{:S(2)}) copy-start(f32[3,8,8,512]{3,2,1,0:T(8,128)} %start.1) | copy-start | bytes 1179652
  3.5 0.9 %copy-start.3 = (s32[8,8,512]{2,1,0:T(8,128)S(1)}, s32[8,8,512]{2,1,0:T(8,128)}, u32[]{:S(2)}) copy-start(s32[8,8,512]{2,1,0:T(8,128)} %mask.1) | copy-start | bytes 393220
  4.4 0.7 %copy-start.4 = (bf16[24,24]{1,0:T(8,128)(2,1)S(1)}, bf16[24,24]{1,0:T(8,128)(2,1)}, u32[]{:S(2)}) copy-start(bf16[24,24]{1,0:T(8,128)(2,1)} %stiff.1) | copy-start | bytes 3460
where the time goes:
time: 38.7 us; the launch traced here: 38.3 us
  Pallas kernels  32.4 us (84%)
  local copies, waits for them, and re-layouts  5.86 us (15%)
    pallas_call x1, Pallas kernels, body(): pl.pallas_call(functools.partial(kernel, where, n_z, n_y), out_shape=jax....  32.4 us
    unnamed x11, local copies, waits for them, and re-layouts  5.86 us

commit v1 on v0

v1 whole, which is shorter than its diff:
```python
import functools

import jax
import jax.numpy as jnp
import ml_dtypes
import numpy as np
from jax import lax
from jax.experimental import pallas as pl
from jax.experimental.pallas import tpu as pltpu
from jax.sharding import PartitionSpec as P

DOF = 3
EDOF = 24
B = 8
C = B // 2
LOW = 0.1
MESH = pl.DeviceIdType.MESH
F32, BF16 = jnp.float32, jnp.bfloat16

NEAR = [(-1, -1), (-1, 1), (1, -1), (1, 1), (0, -1), (0, 1), (-1, 0), (1, 0)]
EDGE = {-1: (0, 3), 0: (0, 5), 1: (2, 3)}
RHS_ROWS = [32, 32, 32, 32, 48, 48, 48, 48]
RHS_AT = [0, 32, 64, 96, 128, 176, 224, 272]
RHS_ALL = 320


def col_code(col):
    if col < 144:
        return col // 48, col % 48 // 24, col % 24 // 8, col % 8
    p, sx, r = (col - 144) // 16, col % 16 // 8, col % 8
    if r < 6:
        return p, sx, r % 3, -1 if r < 3 else 8
    return None


def tables(nx):
    half = nx // 2
    out = {}
    rep = np.zeros((192, EDOF))
    for r in range(192):
        rep[r, (r // 24) * 3 + (r % 24) // 8] = 1
    out["rep"] = rep
    rep_x = np.zeros((64, EDOF))
    for q in range(8):
        for d in range(3):
            rep_x[q * 8 + d, q * 3 + d] = 1
    out["rep_x"] = rep_x
    for cz2 in range(2):
        for cy2 in range(2):
            pick = np.zeros((32, 192))
            keep = np.zeros((192, 192))
            for col in range(192):
                code = col_code(col)
                if code is None:
                    continue
                p, sx, d, y2 = code
                pick[3 * (4 * cz2 + 2 * cy2 + sx) + d, col] = 1
                for r in range(192):
                    q, y = r // 24, r % 8
                    cz, cy = q // 4, (q // 2) % 2
                    if p == 1 - cz + cz2 and y2 == y - cy + cy2:
                        keep[r, col] = 1
            out["pick%d%d" % (cz2, cy2)] = pick
            out["keep%d%d" % (cz2, cy2)] = keep
    sel_y = np.zeros((48, 192))
    for z in range(B):
        for d in range(3):
            sel_y[z * 3 + d, z * 24 + d * 8] = 1
            sel_y[24 + z * 3 + d, z * 24 + d * 8 + 7] = 1
    out["sel_y"] = sel_y
    for b in range(4):
        sel = np.zeros((64, 192))
        put = np.zeros((16, 64))
        for k, (z, y) in enumerate([(0, 0), (0, 7), (7, 0), (7, 7)]):
            for d in range(3):
                sel[16 * k + 3 * b + d, z * 24 + d * 8 + y] = 1
                put[8 * (k // 2) + 3 * (k % 2) + d, 16 * k + 3 * b + d] = 1
        out["sel_c%d" % b] = sel
        out["put_c%d" % b] = put
    for h in range(2):
        put = np.zeros((64, 96))
        for d in range(3):
            for z in range(B):
                put[z * 8 + d, h * 24 + z * 3 + d] = 1
                put[z * 8 + 3 + d, 48 + h * 24 + z * 3 + d] = 1
        out["put_y%d" % h] = put
    mask_sel = np.zeros((48, 64))
    for i in range(8):
        mask_sel[i, 56 + i] = 1
        mask_sel[8 + i, i * 8 + 7] = 1
    mask_sel[16, 63] = 1
    for z in range(B):
        for y in range(B):
            mask_sel[32 + (z // 2) * C + y // 2, z * 8 + y] = 0.25
    out["mask_sel"] = mask_sel
    mask_put = np.zeros((144, 96))
    for layer in range(-1, B):
        for y in range(B):
            for cy in range(2):
                row, y2 = (layer + 1) * 16 + cy * 8 + y, y - cy
                if layer >= 0:
                    mask_put[row, layer * 8 + y2 if y2 >= 0 else 72 + layer] = 1
                else:
                    mask_put[row, 64 + y2 if y2 >= 0 else 80] = 1
    out["mask_put"] = mask_put
    pairs = np.zeros((nx, half))
    down = np.zeros((nx, half))
    for i in range(nx):
        pairs[i, i // 2] = 1
        if i % 2 == 0:
            down[i, i // 2] = 1
        else:
            down[i, i // 2] = 0.5
            if i // 2 + 1 < half:
                down[i, i // 2 + 1] = 0.5
    out["pairs"], out["down"] = pairs, down
    up = down.T
    out["up"] = up
    cs_put = np.zeros((320, 144))

    def place(index):
        return (index + C) // C, (index + C) % C

    for layer in range(-3, 7):
        zs, kz = place(layer)
        base = (layer + 3) * 32
        for t in range(8):
            for cy in range(2):
                ys, ky = place(t - 1 - cy)
                cs_put[base + cy * 8 + t, (zs * 3 + ys) * 16 + kz * C + ky] = 1
        for d in range(3):
            for cy in range(2):
                ys, ky = place(-2 - cy)
                cs_put[base + 16 + cy * 8 + d, (zs * 3 + ys) * 16 + kz * C + ky] = 1
    out["cs_put"] = cs_put
    line = np.zeros((C + 1, B))
    for i in range(B):
        if i % 2 == 0:
            line[i // 2, i] = 1
        else:
            line[i // 2, i] = 0.5
            line[i // 2 + 1, i] = 0.5
    shrink = np.zeros((80, 192))
    grow = np.zeros((192, 120))
    for k in range(C + 1):
        for j in range(C + 1):
            for z in range(B):
                for y in range(B):
                    for d in range(3):
                        w = line[k, z] * line[j, y]
                        shrink[k * 16 + j * 3 + d, z * 24 + d * 8 + y] = w
                        grow[z * 24 + d * 8 + y, k * 24 + d * 8 + j + 1] = w
    out["shrink"], out["grow"] = shrink, grow
    hand = np.zeros((RHS_ALL, 80))
    gather = np.zeros((288, RHS_ALL + 160))

    def message(dz, dy):
        (z0, nz), (y0, ny) = EDGE[dz], EDGE[dy]
        return [(k, y, d) for k in range(z0, z0 + nz) for y in range(y0, y0 + ny) for d in range(3)]

    for n, (dz, dy) in enumerate(NEAR):
        for i, (k, y, d) in enumerate(message(dz, dy)):
            hand[RHS_AT[n] + i, k * 16 + y * 3 + d] = 1
    sources = [(RHS_AT[n], dz, dy, message(-dz, -dy)) for n, (dz, dy) in enumerate(NEAR)]
    own = {(k, y, d): k * 16 + y * 3 + d for k in range(5) for y in range(5) for d in range(3)}
    for at, dz, dy, rows in sources:
        for i, (k, y, d) in enumerate(rows):
            k2, y2 = k + C * dz, y + C * dy
            if -2 <= k2 <= 6 and -1 <= y2 <= 6:
                gather[(k2 + 2) * 32 + d * 8 + y2 + 1, at + i] = 1
            if -2 <= k2 <= 6 and y2 == -2:
                gather[(k2 + 2) * 32 + 24 + d, at + i] = 1
    for (k, y, d), i in own.items():
        for at in (RHS_ALL, RHS_ALL + 80):
            gather[(k + 2) * 32 + d * 8 + y + 1, at + i] = 1
    out["hand"], out["gather"] = hand, gather
    return out


EARLY = ["sel_y", "sel_c0", "sel_c1", "sel_c2", "sel_c3", "mask_sel"]


def pack_tables(nx):
    all_tables = tables(nx)
    wide = [n for n, v in all_tables.items() if v.shape[1] > 256]
    rest = [n for n in all_tables if n not in EARLY and n not in wide]
    where, packed = {}, []
    for group, names in enumerate((EARLY, rest, wide)):
        width = max(all_tables[n].shape[1] for n in names)
        width = -(-width // 128) * 128
        parts, at = [], 0
        for name in names:
            rows, cols = all_tables[name].shape
            where[name] = (group, at, rows, cols)
            tall = -(-rows // 16) * 16
            padded = np.zeros((tall, width), np.float32)
            padded[:rows, :cols] = all_tables[name]
            parts.append(padded)
            at += tall
        packed.append(np.concatenate(parts).astype(ml_dtypes.bfloat16))
    return where, packed


def kernel(where, n_z, n_y, load_h, start_h, mask_h, stiff_h, tab0_h, tab1_h, tab2_h, out, load, start, mask, stiff, tab0, tab1, tab2,
           xs, upd, inv, idle, ss, vb, vh, sw, sc, rw, rc, mr, ms, cs, cr, rsend_buf, rr, cx, cu, cinv, cidle, css, crhs, cvb, cvh,
           wmat, local_sem, send_sem, recv_sem, msend, mrecv, csend, crecv, rsend, rrecv):
    nx = load.shape[-1]
    half, quarter = nx // 2, nx // 4
    gz, gy = lax.axis_index("gz"), lax.axis_index("gy")
    moves = {}
    for k, (name, src, dst) in enumerate([("start", start_h, start), ("tab0", tab0_h, tab0), ("mask", mask_h, mask), ("tab1", tab1_h, tab1),
                                          ("stiff", stiff_h, stiff), ("load", load_h, load), ("tab2", tab2_h, tab2)]):
        moves[name] = pltpu.make_async_copy(src, dst, local_sem.at[k])
        moves[name].start()

    def t(name, rows=None):
        group, at, r, c = where[name]
        return (tab0, tab1, tab2)[group][at : at + (rows or r), :c]

    def dot(a, b):
        return jnp.dot(a, b, preferred_element_type=F32)

    def exists(dz, dy):
        ok = None
        for delta, pos, n in ((dz, gz, n_z), (dy, gy, n_y)):
            if delta:
                test = pos > 0 if delta < 0 else pos < n - 1
                ok = test if ok is None else jnp.logical_and(ok, test)
        return ok

    mask_to = [(1, 0), (0, 1), (1, 1)]
    barrier = pltpu.get_barrier_semaphore()
    count = 0
    for dz, dy in NEAR:
        ok = exists(dz, dy)
        count = count + ok.astype(jnp.int32)

        @pl.when(ok)
        def _():
            pl.semaphore_signal(barrier, inc=1, device_id=(gz + dz, gy + dy), device_id_type=MESH)

    for k, (dz, dy) in enumerate(NEAR):

        @pl.when(jnp.logical_not(exists(dz, dy)))
        def _():
            if k < 4:
                rc[:, 16 * k : 16 * k + 16] = jnp.zeros((4, 16, quarter), BF16)
            else:
                rw[:, k - 4] = jnp.zeros((4, 48, half), BF16)
            slot = ((dz + 1) * 3 + dy + 1) * 16
            cr[slot : slot + 16] = jnp.zeros((16, half), BF16)
            if (-dz, -dy) in mask_to:
                mr[mask_to.index((-dz, -dy))] = jnp.zeros((16, half), BF16)
            rr[RHS_AT[k] : RHS_AT[k] + RHS_ROWS[k]] = jnp.zeros((RHS_ROWS[k], half), BF16)

    def push(src, dst, send, recv, k):
        dz, dy = NEAR[k]
        return pltpu.make_async_remote_copy(
            src_ref=src, dst_ref=dst, send_sem=send, recv_sem=recv, device_id=(gz + dz, gy + dy), device_id_type=MESH)

    def back(k):
        return NEAR.index((-NEAR[k][0], -NEAR[k][1]))

    def field_copy(p, k):
        j = back(k)
        if k < 4:
            src, dst = sc.at[p, 16 * k : 16 * k + 16], rc.at[p, 16 * j : 16 * j + 16]
        else:
            src, dst = sw.at[p, k - 4], rw.at[p, j - 4]
        return push(src, dst, send_sem.at[p, k], recv_sem.at[p, j], k)

    def mask_copy(m):
        return push(ms.at[m], mr.at[m], msend.at[m], mrecv.at[m], NEAR.index(mask_to[m]))

    def scale_copy(k):
        dz, dy = NEAR[k]
        to = ((1 - dz) * 3 + 1 - dy) * 16
        return push(cs, cr.at[to : to + 16], csend.at[k], crecv.at[back(k)], k)

    def rhs_copy(k):
        j, n = back(k), RHS_ROWS[k]
        return push(rsend_buf.at[RHS_AT[k] : RHS_AT[k] + n], rr.at[RHS_AT[j] : RHS_AT[j] + n], rsend.at[k], rrecv.at[j], k)

    def halves(v):
        return jnp.concatenate([v[:, :half], v[:, half:]], axis=0)

    def joined(v):
        n = v.shape[0] // 2
        return jnp.concatenate([v[:n], v[n:]], axis=1)

    def pack_field(p, planes):
        own = jnp.concatenate(planes, axis=0).astype(BF16)
        corner = None
        for b in range(4):
            term = dot(t("sel_c%d" % b), own[:, b * quarter : (b + 1) * quarter])
            corner = term if corner is None else corner + term
        sc[p] = corner.astype(BF16)
        rows = dot(t("sel_y"), own)
        sw[p, 0] = halves(rows[0:24]).astype(BF16)
        sw[p, 1] = halves(rows[24:48]).astype(BF16)
        sw[p, 2] = halves(jnp.concatenate(planes[0:3], axis=0)).astype(BF16)
        sw[p, 3] = halves(jnp.concatenate(planes[21:24], axis=0)).astype(BF16)

    def each(copy, do, ks=range(8)):
        for k in ks:

            @pl.when(exists(*NEAR[k]))
            def _():
                do(copy(k))

    def begin(c):
        c.start()

    def arrived(copy):
        each(lambda k: copy(back(k)), lambda c: c.wait_recv())

    moves["start"].wait()
    moves["tab0"].wait()
    pack_field(0, [start[d, z] for z in range(B) for d in range(3)])
    moves["mask"].wait()
    mask_wide = jnp.concatenate([mask[z] for z in range(B)], axis=0).astype(F32)
    picked = dot(t("mask_sel"), mask_wide.astype(BF16))
    for m in range(3):
        ms[m] = halves(picked[8 * m : 8 * m + 8]).astype(BF16)

    pl.semaphore_wait(barrier, count)
    each(lambda k: field_copy(0, k), begin)
    for m in range(3):

        @pl.when(exists(*mask_to[m]))
        def _():
            mask_copy(m).start()

    moves["tab1"].wait()
    moves["stiff"].wait()
    stiff_bf = stiff[...]
    stiff_wide = stiff_bf.astype(F32)
    eye = lax.broadcasted_iota(jnp.int32, (EDOF, EDOF), 0) == lax.broadcasted_iota(jnp.int32, (EDOF, EDOF), 1)
    diag_mat = jnp.where(eye, stiff_wide, 0.0)
    bound = jnp.max(jnp.sum(jnp.abs(stiff_wide), axis=1, keepdims=True) / jnp.sum(diag_mat, axis=1, keepdims=True), axis=0, keepdims=True)
    rows_of = dot(t("rep"), stiff_bf).astype(BF16)
    total = None
    for cz2 in range(2):
        for cy2 in range(2):
            name = "%d%d" % (cz2, cy2)
            term = dot(rows_of, t("pick" + name, EDOF)) * t("keep" + name).astype(F32)
            total = term if total is None else total + term
    wmat[...] = total.astype(BF16)
    diag_bf = diag_mat.astype(BF16)
    diag_col = jnp.sum(dot(t("rep"), diag_bf), axis=1, keepdims=True)
    diag_col_x = jnp.sum(dot(t("rep_x"), diag_bf), axis=1, keepdims=True)

    def shift_up(v):
        lane = lax.broadcasted_iota(jnp.int32, v.shape, 1)
        return jnp.where(lane == 0, 0.0, pltpu.roll(v, 1, axis=1))

    def shift_down(v):
        n = v.shape[1]
        lane = lax.broadcasted_iota(jnp.int32, v.shape, 1)
        return jnp.where(lane == n - 1, 0.0, pltpu.roll(v, n - 1, axis=1))

    def diagonal(scale, z, d):
        sums = []
        for c in range(2):
            s = None
            for cz in range(2):
                for cy in range(2):
                    at = (4 * cz + 2 * cy + c) * 24 + d * 8
                    term = diag_col[at : at + 8] * scale(z - cz, cy)
                    s = term if s is None else s + term
            sums.append(s)
        return sums[0] + shift_up(sums[1])

    def apply(planes, scale_now, scale_below):
        terms = dot(wmat[...], planes)
        sums = []
        for c in range(2):
            parts = []
            for d in range(3):
                s = None
                for cz, sc in ((0, scale_now), (1, scale_below)):
                    for cy in range(2):
                        at = (4 * cz + 2 * cy + c) * 24 + d * 8
                        term = terms[at : at + 8] * sc[cy * 8 : cy * 8 + 8]
                        s = term if s is None else s + term
                parts.append(s)
            sums.append(jnp.concatenate(parts, axis=0))
        return sums[0] + shift_up(sums[1])

    def put_plane(ref, z, rows):
        ref[z] = jnp.concatenate([rows, shift_down(rows)], axis=0).astype(BF16)

    def build_own(x_of):
        for z in range(B):
            put_plane(vb, z + 1, jnp.concatenate([x_of(z, d) for d in range(3)], axis=0))

    def build_halo(p):
        sides = rw[p, 0:2].reshape(96, half)
        inner = jnp.concatenate([dot(t("put_y%d" % h), sides) for h in range(2)], axis=1)
        ends = jnp.concatenate([dot(t("put_c%d" % b), rc[p]) for b in range(4)], axis=1)
        for z in range(B):
            put_plane(vh, z + 1, inner[8 * z : 8 * z + 8])
        for k, z in enumerate((0, B + 1)):
            put_plane(vh, z, ends[8 * k : 8 * k + 8])
            put_plane(vb, z, joined(rw[p, 2 + k].astype(F32)))

    def planes_of(own, edge, z, n):
        return jnp.concatenate([own[pl.ds(z, 3)].reshape(144, n), edge[pl.ds(z, 3)].reshape(48, n)], axis=0)

    build_own(lambda z, d: start[d, z])
    cs[...] = dot(picked[32:48].astype(BF16), t("pairs")).astype(BF16)
    cr[64:80] = cs[...]

    for m in range(3):

        @pl.when(exists(-mask_to[m][0], -mask_to[m][1]))
        def _():
            mask_copy(m).wait_recv()

    came = [joined(mr[m].astype(F32)) for m in range(3)]
    all_masks = jnp.concatenate([mask_wide] + came + [jnp.zeros((8, nx), F32)], axis=0).astype(BF16)
    ss[...] = dot(t("mask_put"), all_masks).reshape(B + 1, 16, nx)

    def prepare(z, carry):
        for d in range(3):
            dg = diagonal(lambda layer, cy: ss[layer + 1, cy * 8 : cy * 8 + 8], z, d)
            no = jnp.where(dg == 0.0, 1.0, 0.0)
            inv[z, d * 8 : d * 8 + 8] = 1.0 / ((dg + no) * bound)
            if d == 0:
                idle[z] = no
        return carry

    lax.fori_loop(0, B, prepare, 0)

    ratio = (1.0 + LOW) / (1.0 - LOW)
    rho = [1.0 / ratio]
    for _ in range(2):
        rho.append(1.0 / (2.0 * ratio - rho[-1]))
    steps = [(0.0, 1.0 / (0.5 * (1.0 + LOW)))]
    for i in range(2):
        steps.append((rho[i + 1] * rho[i], 2.0 * rho[i + 1] / (0.5 * (1.0 - LOW))))

    def stack(ref, z):
        return jnp.concatenate([ref[0, z], ref[1, z], ref[2, z]], axis=0)

    def three(v):
        return jnp.concatenate([v, v, v], axis=0)

    moves["load"].wait()
    moves["tab2"].wait()
    for p in range(4):
        if p > 0:
            pack_field(p, [xs[z, 8 * d : 8 * d + 8] for z in range(B) for d in range(3)])
            each(lambda k: field_copy(p, k), begin)
            if p == 1:
                each(scale_copy, begin)
            build_own(lambda z, d: xs[z, 8 * d : 8 * d + 8])
        arrived(lambda k: field_copy(p, k))
        build_halo(p)

        def plane(z):
            x = stack(start, z) if p == 0 else xs[z]
            kv = apply(planes_of(vb, vh, z, nx), ss[z + 1], ss[z])
            r = stack(load, z) - kv - three(idle[z]) * x
            if p < 3:
                u = steps[p][1] * inv[z] * r
                if p > 0:
                    u = u + steps[p][0] * upd[z]
                xs[z] = x + u
                upd[z] = u
            else:
                upd[z] = r

        def two(i, carry):
            for j in range(4):
                plane(4 * i + j)
            return carry

        lax.fori_loop(0, B // 4, two, 0)

    def split(v):
        hi = v.astype(BF16)
        return hi, (v - hi.astype(F32)).astype(BF16)

    hi, lo = split(upd[...].reshape(192, nx))
    narrow = dot(t("shrink"), hi) + dot(t("shrink"), lo)
    hi, lo = split(narrow)
    partial = dot(hi, t("down")) + dot(lo, t("down"))
    hi, lo = split(partial)
    rsend_buf[...] = dot(t("hand"), hi).astype(BF16)
    each(rhs_copy, begin)
    rr[RHS_ALL : RHS_ALL + 80] = hi
    rr[RHS_ALL + 80 : RHS_ALL + 160] = lo

    arrived(scale_copy)
    css[...] = dot(t("cs_put"), cr[...]).reshape(10, 32, half)
    last_z, last_y = gz == n_z - 1, gy == n_y - 1
    row8 = lax.broadcasted_iota(jnp.int32, (8, half), 0)
    good_y = jnp.where(jnp.logical_and(last_y, row8 >= C + 1), 0.0, 1.0)
    for k in range(9):
        good = good_y
        if k - 2 >= C:
            good = good * jnp.where(last_z, 0.0, 1.0)
        for d in range(3):
            dg = diagonal(lambda layer, cy: css[layer + 1, cy * 8 : cy * 8 + 8], k, d)
            no = jnp.where(dg == 0.0, 1.0, 0.0)
            cinv[k, d * 8 : d * 8 + 8] = good / ((dg + no) * bound)
            if d == 0:
                cidle[k] = no
        sums = []
        for c in range(2):
            s = None
            for cz in range(2):
                for cy in range(2):
                    at = (4 * cz + 2 * cy + c) * 8
                    term = diag_col_x[at : at + 8] * css[k + 1 - cz, 16 + cy * 8 : 24 + cy * 8]
                    s = term if s is None else s + term
            sums.append(s)
        dg = sums[0] + shift_up(sums[1])
        no = jnp.where(dg == 0.0, 1.0, 0.0)
        extra = 1.0 / ((dg + no) * bound)
        if k - 2 >= C:
            extra = extra * jnp.where(last_z, 0.0, 1.0)
        cinv[k, 24:32] = extra

    arrived(rhs_copy)
    right = dot(t("gather"), rr[...])
    for k in range(9):
        total = right[32 * k : 32 * k + 32]
        crhs[k] = total[0:24]
        x = steps[0][1] * cinv[k] * total
        cx[k] = x[0:24]
        cu[k] = x[0:24]
        put_plane(cvb, k, x[0:24])
        put_plane(cvh, k, x[24:32])

    for p, (first, last) in ((1, (1, 7)), (2, (2, 6))):
        for k in range(first, last + 1):
            kv = apply(planes_of(cvb, cvh, k - 1, half), css[k + 1], css[k])
            x = cx[k]
            r = crhs[k] - kv - three(cidle[k]) * x
            u = steps[p][0] * cu[k] + steps[p][1] * cinv[k, 0:24] * r
            cx[k] = x + u
            cu[k] = u
        if p == 1:
            for k in range(first, last + 1):
                put_plane(cvb, k, cx[k])
                cvh[k] = jnp.zeros((16, half), BF16)

    fix = cx[2:7].reshape(120, half).astype(BF16)
    hi, lo = split(dot(t("grow"), fix))
    side = dot(hi, t("up")) + dot(lo, t("up"))
    for z in range(B):
        for d in range(3):
            at = z * 24 + d * 8
            out[d, z] = xs[z, 8 * d : 8 * d + 8] + side[at : at + 8]

    for p in range(4):
        each(lambda k: field_copy(p, k), lambda c: c.wait_send())
    each(scale_copy, lambda c: c.wait_send())
    each(rhs_copy, lambda c: c.wait_send())
    for m in range(3):

        @pl.when(exists(*mask_to[m]))
        def _():
            mask_copy(m).wait_send()


def body(n_z, n_y, load, start, mask, stiff):
    nx = load.shape[-1]
    half, quarter = nx // 2, nx // 4
    where, packed = pack_tables(nx)
    given = [load, start, mask, stiff] + [jnp.asarray(v) for v in packed]
    dma = pltpu.SemaphoreType.DMA
    vmem = pl.BlockSpec(memory_space=pltpu.VMEM)
    hbm = pl.BlockSpec(memory_space=pltpu.HBM)
    return pl.pallas_call(
        functools.partial(kernel, where, n_z, n_y),
        out_shape=jax.ShapeDtypeStruct(load.shape, F32),
        in_specs=[hbm] * len(given),
        out_specs=vmem,
        scratch_shapes=[pltpu.VMEM(v.shape, v.dtype) for v in given]
        + [
            pltpu.VMEM((B, 24, nx), F32),
            pltpu.VMEM((B, 24, nx), F32),
            pltpu.VMEM((B, 24, nx), F32),
            pltpu.VMEM((B, 8, nx), F32),
            pltpu.VMEM((B + 1, 16, nx), F32),
            pltpu.VMEM((B + 2, 48, nx), BF16),
            pltpu.VMEM((B + 2, 16, nx), BF16),
            pltpu.VMEM((4, 4, 48, half), BF16),
            pltpu.VMEM((4, 64, quarter), BF16),
            pltpu.VMEM((4, 4, 48, half), BF16),
            pltpu.VMEM((4, 64, quarter), BF16),
            pltpu.VMEM((3, 16, half), BF16),
            pltpu.VMEM((3, 16, half), BF16),
            pltpu.VMEM((16, half), BF16),
            pltpu.VMEM((144, half), BF16),
            pltpu.VMEM((RHS_ALL, half), BF16),
            pltpu.VMEM((RHS_ALL + 160, half), BF16),
            pltpu.VMEM((9, 24, half), F32),
            pltpu.VMEM((9, 24, half), F32),
            pltpu.VMEM((9, 32, half), F32),
            pltpu.VMEM((9, 8, half), F32),
            pltpu.VMEM((10, 32, half), F32),
            pltpu.VMEM((9, 24, half), F32),
            pltpu.VMEM((9, 48, half), BF16),
            pltpu.VMEM((9, 16, half), BF16),
            pltpu.VMEM((192, 192), BF16),
            dma((7,)), dma((4, 8)), dma((4, 8)), dma((3,)), dma((3,)), dma((8,)), dma((8,)), dma((8,)), dma((8,)),
        ],
        compiler_params=pltpu.CompilerParams(collective_id=0, has_side_effects=True, vmem_limit_bytes=48 * 1024 * 1024),
    )(*given)


def solution(mesh):
    in_specs = (P(None, "gz", "gy", None), P(None, "gz", "gy", None), P("gz", "gy", None), P())
    out_specs = P(None, "gz", "gy", None)
    fn = functools.partial(body, mesh.shape["gz"], mesh.shape["gy"])
    return jax.shard_map(fn, mesh=mesh, in_specs=in_specs, out_specs=out_specs, check_vma=False)
```

time: 38.7 us -> 38.8 us (level)
  local copies, waits for them, and re-layouts: 5.86 us -> 7.78 us
  Pallas kernels: 32.4 us -> 30.6 us
    unnamed x11 -> x15, local copies, waits for them, and re-layouts: 5.86 us -> 7.78 us
    pallas_call x1, Pallas kernels: 32.4 us -> 30.6 us  [body(): pl.pallas_call(functools.partial(kernel, where, n_z, n_y), out_shape=jax....]
where the time goes in v1:
time: 38.8 us; the launch traced here: 38.4 us
  Pallas kernels  30.6 us (79%)
  local copies, waits for them, and re-layouts  7.78 us (20%)
    pallas_call x1, Pallas kernels, body(): pl.pallas_call(functools.partial(kernel, where, n_z, n_y), out_shape=jax....  30.6 us
    unnamed x15, local copies, waits for them, and re-layouts  7.78 us

profile of v1, /device:TPU:3, one launch (start us, length us, event | category | flops | bytes accessed | tf_op | source)
XLA Modules:
  0.0 38.4 jit_solution(17331993741297830496)
XLA Ops:
  0.0 0.0 copy-start
  0.0 1.5 %copy-done = bf16[3424,256]{1,0:T(8,128)(2,1)S(1)} copy-done((bf16[3424,256]{1,0:T(8,128)(2,1)S(1)}, bf16[3424,256]{1,0:T(8,128)(2,1)}, u32[]{:S(2)}) %copy-start) | copy-done | bytes 1753112
  1.5 0.0 copy-start.1
  1.5 1.1 %copy-done.1 = bf16[544,512]{1,0:T(8,128)(2,1)S(1)} copy-done((bf16[544,512]{1,0:T(8,128)(2,1)S(1)}, bf16[544,512]{1,0:T(8,128)(2,1)}, u32[]{:S(2)}) %copy-start.1) | copy-done | bytes 557080
  2.5 0.0 copy-start.2
  2.5 1.0 %copy-done.2 = f32[3,8,8,512]{3,2,1,0:T(8,128)S(1)} copy-done((f32[3,8,8,512]{3,2,1,0:T(8,128)S(1)}, f32[3,8,8,512]{3,2,1,0:T(8,128)}, u32[]{:S(2)}) %copy-start.2) | copy-done | bytes 393240
  3.5 0.0 copy-start.3
  3.5 1.0 %copy-done.3 = f32[3,8,8,512]{3,2,1,0:T(8,128)S(1)} copy-done((f32[3,8,8,512]{3,2,1,0:T(8,128)S(1)}, f32[3,8,8,512]{3,2,1,0:T(8,128)}, u32[]{:S(2)}) %copy-start.3) | copy-done | bytes 393240
  4.5 0.0 copy-start.4
  4.5 0.9 %copy-done.4 = bf16[352,256]{1,0:T(8,128)(2,1)S(1)} copy-done((bf16[352,256]{1,0:T(8,128)(2,1)S(1)}, bf16[352,256]{1,0:T(8,128)(2,1)}, u32[]{:S(2)}) %copy-start.4) | copy-done | bytes 180248
  5.4 0.0 copy-start.5
  5.4 0.9 %copy-done.5 = s32[8,8,512]{2,1,0:T(8,128)S(1)} copy-done((s32[8,8,512]{2,1,0:T(8,128)S(1)}, s32[8,8,512]{2,1,0:T(8,128)}, u32[]{:S(2)}) %copy-start.5) | copy-done | bytes 131096
  6.3 0.0 copy-start.6
  6.3 0.7 %copy-done.6 = bf16[24,24]{1,0:T(8,128)(2,1)S(1)} copy-done((bf16[24,24]{1,0:T(8,128)(2,1)S(1)}, bf16[24,24]{1,0:T(8,128)(2,1)}, u32[]{:S(2)}) %copy-start.6) | copy-done | bytes 1176
  7.0 30.6 %shard_map.73 = f32[3,8,8,512]{3,2,1,0:T(8,128)S(1)} custom-call(f32[3,8,8,512]{3,2,1,0:T(8,128)S(1)} %copy-done.2, f32[3,8,8,512]{3,2,1,0:T(8,128)S(1)} %copy-done.3, s32[8,8,512]{2,1,0:T(8,128)S(1)} %copy-done.5, bf16[24,24]{1,0:T(8,128)(2,1)S(1)} %copy-done.6, bf16[352,256]{1,0:T(8,128)(2,1)S(1)} %copy-done.4, bf16[3424,256]{1,0:T(8,128)(2,1)S(1)} %copy-done, ...), custom_call_target="tpu_custom_call" | custom-call | tf_op jit(solution)/shard_map/pallas_call | solution.py:577
  37.7 0.7 %copy.9 = f32[3,8,8,512]{3,2,1,0:T(8,128)} copy(f32[3,8,8,512]{3,2,1,0:T(8,128)S(1)} %shard_map.73) | data formatting | bytes 786432
Async XLA Ops:
  0.0 1.5 %copy-start = (bf16[3424,256]{1,0:T(8,128)(2,1)S(1)}, bf16[3424,256]{1,0:T(8,128)(2,1)}, u32[]{:S(2)}) copy-start(bf16[3424,256]{1,0:T(8,128)(2,1)} %constant.7.clone.tab1_h) | copy-start | bytes 5259268
  1.5 1.1 %copy-start.1 = (bf16[544,512]{1,0:T(8,128)(2,1)S(1)}, bf16[544,512]{1,0:T(8,128)(2,1)}, u32[]{:S(2)}) copy-start(bf16[544,512]{1,0:T(8,128)(2,1)} %constant.8.clone.tab2_h) | copy-start | bytes 1671172
  2.5 1.0 %copy-start.2 = (f32[3,8,8,512]{3,2,1,0:T(8,128)S(1)}, f32[3,8,8,512]{3,2,1,0:T(8,128)}, u32[]{:S(2)}) copy-start(f32[3,8,8,512]{3,2,1,0:T(8,128)} %load_h.1) | copy-start | bytes 1179652
  3.5 1.0 %copy-start.3 = (f32[3,8,8,512]{3,2,1,0:T(8,128)S(1)}, f32[3,8,8,512]{3,2,1,0:T(8,128)}, u32[]{:S(2)}) copy-start(f32[3,8,8,512]{3,2,1,0:T(8,128)} %start_h.1) | copy-start | bytes 1179652
  4.5 0.9 %copy-start.4 = (bf16[352,256]{1,0:T(8,128)(2,1)S(1)}, bf16[352,256]{1,0:T(8,128)(2,1)}, u32[]{:S(2)}) copy-start(bf16[352,256]{1,0:T(8,128)(2,1)} %constant.6.clone.tab0_h) | copy-start | bytes 540676
  5.4 0.9 %copy-start.5 = (s32[8,8,512]{2,1,0:T(8,128)S(1)}, s32[8,8,512]{2,1,0:T(8,128)}, u32[]{:S(2)}) copy-start(s32[8,8,512]{2,1,0:T(8,128)} %mask_h.1) | copy-start | bytes 393220
  6.3 0.7 %copy-start.6 = (bf16[24,24]{1,0:T(8,128)(2,1)S(1)}, bf16[24,24]{1,0:T(8,128)(2,1)}, u32[]{:S(2)}) copy-start(bf16[24,24]{1,0:T(8,128)(2,1)} %stiff_h.1) | copy-start | bytes 3460

commit v2 on v1

--- a/solution.py
+++ b/solution.py
@@ -62,28 +62,35 @@
                         keep[r, col] = 1
             out["pick%d%d" % (cz2, cy2)] = pick
             out["keep%d%d" % (cz2, cy2)] = keep
-    sel_y = np.zeros((48, 192))
-    for z in range(B):
-        for d in range(3):
-            sel_y[z * 3 + d, z * 24 + d * 8] = 1
-            sel_y[24 + z * 3 + d, z * 24 + d * 8 + 7] = 1
-    out["sel_y"] = sel_y
-    for b in range(4):
-        sel = np.zeros((64, 192))
-        put = np.zeros((16, 64))
-        for k, (z, y) in enumerate([(0, 0), (0, 7), (7, 0), (7, 7)]):
-            for d in range(3):
-                sel[16 * k + 3 * b + d, z * 24 + d * 8 + y] = 1
-                put[8 * (k // 2) + 3 * (k % 2) + d, 16 * k + 3 * b + d] = 1
-        out["sel_c%d" % b] = sel
-        out["put_c%d" % b] = put
-    for h in range(2):
-        put = np.zeros((64, 96))
-        for d in range(3):
-            for z in range(B):
-                put[z * 8 + d, h * 24 + z * 3 + d] = 1
-                put[z * 8 + 3 + d, 48 + h * 24 + z * 3 + d] = 1
-        out["put_y%d" % h] = put
+    sel = np.zeros((80, 192))
+    for d in range(3):
+        for z in range(B):
+            sel[z * 3 + d, z * 24 + d * 8] = 1
+            sel[24 + z * 3 + d, z * 24 + d * 8 + 7] = 1
+        for k, (dz, dy) in enumerate(NEAR[:4]):
+            z, y = 7 if dz > 0 else 0, 7 if dy > 0 else 0
+            sel[48 + 8 * k + (0 if dz > 0 else 3) + d, z * 24 + d * 8 + y] = 1
+    out["sel"] = sel
+    rep_y = np.zeros((192, EDOF))
+    rows_y = []
+    for r in range(192):
+        side, cz, cx, d, z = r // 96, r // 48 % 2, r // 24 % 2, r // 8 % 3, r % 8
+        rep_y[r, 3 * (4 * cz + 2 * (1 - side) + cx) + d] = 1
+        rows_y.append((side, cz, z))
+    out["rep_y"] = rep_y
+    for cz2 in range(2):
+        pick = np.zeros((32, 128))
+        keep = np.zeros((192, 128))
+        for col in range(128):
+            side, sx, rc = col // 64, col // 32 % 2, col % 32
+            if rc >= 30:
+                continue
+            z2 = rc // 3 if rc < 24 else (-1 if rc < 27 else 8)
+            pick[3 * (4 * cz2 + 2 * side + sx) + rc % 3, col] = 1
+            for r, (row_side, cz, z) in enumerate(rows_y):
+                if row_side == side and z2 == z - cz + cz2:
+                    keep[r, col] = 1
+        out["pick_y%d" % cz2], out["keep_y%d" % cz2] = pick, keep
     mask_sel = np.zeros((48, 64))
     for i in range(8):
         mask_sel[i, 56 + i] = 1
@@ -93,7 +100,12 @@
         for y in range(B):
             mask_sel[32 + (z // 2) * C + y // 2, z * 8 + y] = 0.25
     out["mask_sel"] = mask_sel
-    mask_put = np.zeros((144, 96))
+    mask_put = np.zeros((176, 96))
+    for z in range(B):
+        for cz in range(2):
+            layer = z - cz
+            mask_put[144 + cz * 8 + z, 72 + layer if layer >= 0 else 80] = 1
+            mask_put[160 + cz * 8 + z, layer * 8 + 7 if layer >= 0 else 71] = 1
     for layer in range(-1, B):
         for y in range(B):
             for cy in range(2):
@@ -177,7 +189,7 @@
     return out
 
 
-EARLY = ["sel_y", "sel_c0", "sel_c1", "sel_c2", "sel_c3", "mask_sel"]
+EARLY = ["sel", "mask_sel"]
 
 
 def pack_tables(nx):
@@ -202,8 +214,8 @@
 
 
 def kernel(where, n_z, n_y, load_h, start_h, mask_h, stiff_h, tab0_h, tab1_h, tab2_h, out, load, start, mask, stiff, tab0, tab1, tab2,
-           xs, upd, inv, idle, ss, vb, vh, sw, sc, rw, rc, mr, ms, cs, cr, rsend_buf, rr, cx, cu, cinv, cidle, css, crhs, cvb, cvh,
-           wmat, local_sem, send_sem, recv_sem, msend, mrecv, csend, crecv, rsend, rrecv):
+           xs, upd, inv, idle, res, edge, ss, se, vb, sw, sc, rw, rc, mr, ms, cs, cr, rsend_buf, rr, cx, cu, cinv, cidle, css, crhs, cvb, cvh,
+           wmat, wside, local_sem, send_sem, recv_sem, msend, mrecv, csend, crecv, rsend, rrecv):
     nx = load.shape[-1]
     half, quarter = nx // 2, nx // 4
     gz, gy = lax.axis_index("gz"), lax.axis_index("gy")
@@ -244,7 +256,7 @@
         @pl.when(jnp.logical_not(exists(dz, dy)))
         def _():
             if k < 4:
-                rc[:, 16 * k : 16 * k + 16] = jnp.zeros((4, 16, quarter), BF16)
+                rc[:, k] = jnp.zeros((4, 32, quarter), BF16)
             else:
                 rw[:, k - 4] = jnp.zeros((4, 48, half), BF16)
             slot = ((dz + 1) * 3 + dy + 1) * 16
@@ -264,7 +276,7 @@
     def field_copy(p, k):
         j = back(k)
         if k < 4:
-            src, dst = sc.at[p, 16 * k : 16 * k + 16], rc.at[p, 16 * j : 16 * j + 16]
+            src, dst = sc.at[p, k], rc.at[p, j]
         else:
             src, dst = sw.at[p, k - 4], rw.at[p, j - 4]
         return push(src, dst, send_sem.at[p, k], recv_sem.at[p, j], k)
@@ -290,12 +302,10 @@
 
     def pack_field(p, planes):
         own = jnp.concatenate(planes, axis=0).astype(BF16)
-        corner = None
-        for b in range(4):
-            term = dot(t("sel_c%d" % b), own[:, b * quarter : (b + 1) * quarter])
-            corner = term if corner is None else corner + term
-        sc[p] = corner.astype(BF16)
-        rows = dot(t("sel_y"), own)
+        rows = dot(t("sel"), own)
+        for k in range(4):
+            v = rows[48 + 8 * k : 56 + 8 * k]
+            sc[p, k] = jnp.concatenate([v[:, b * quarter : (b + 1) * quarter] for b in range(4)], axis=0).astype(BF16)
         sw[p, 0] = halves(rows[0:24]).astype(BF16)
         sw[p, 1] = halves(rows[24:48]).astype(BF16)
         sw[p, 2] = halves(jnp.concatenate(planes[0:3], axis=0)).astype(BF16)
@@ -324,12 +334,13 @@
         ms[m] = halves(picked[8 * m : 8 * m + 8]).astype(BF16)
 
     pl.semaphore_wait(barrier, count)
-    each(lambda k: field_copy(0, k), begin)
     for m in range(3):
 
         @pl.when(exists(*mask_to[m]))
         def _():
             mask_copy(m).start()
+
+    each(lambda k: field_copy(0, k), begin)
 
     moves["tab1"].wait()
     moves["stiff"].wait()
@@ -346,6 +357,12 @@
             term = dot(rows_of, t("pick" + name, EDOF)) * t("keep" + name).astype(F32)
             total = term if total is None else total + term
     wmat[...] = total.astype(BF16)
+    rows_of = dot(t("rep_y"), stiff_bf).astype(BF16)
+    total = None
+    for cz2 in range(2):
+        term = dot(rows_of, t("pick_y%d" % cz2, EDOF)) * t("keep_y%d" % cz2).astype(F32)
+        total = term if total is None else total + term
+    wside[...] = total.astype(BF16)
     diag_bf = diag_mat.astype(BF16)
     diag_col = jnp.sum(dot(t("rep"), diag_bf), axis=1, keepdims=True)
     diag_col_x = jnp.sum(dot(t("rep_x"), diag_bf), axis=1, keepdims=True)
@@ -371,43 +388,57 @@
             sums.append(s)
         return sums[0] + shift_up(sums[1])
 
-    def apply(planes, scale_now, scale_below):
-        terms = dot(wmat[...], planes)
+    def put_plane(ref, z, rows):
+        ref[z] = jnp.concatenate([rows, shift_down(rows)], axis=0).astype(BF16)
+
+    def sums_of(terms, scales):
         sums = []
         for c in range(2):
             parts = []
             for d in range(3):
                 s = None
-                for cz, sc in ((0, scale_now), (1, scale_below)):
-                    for cy in range(2):
-                        at = (4 * cz + 2 * cy + c) * 24 + d * 8
-                        term = terms[at : at + 8] * sc[cy * 8 : cy * 8 + 8]
-                        s = term if s is None else s + term
+                for g, sc_g in enumerate(scales):
+                    at = (2 * g + c) * 24 + d * 8
+                    term = terms[at : at + 8] * sc_g
+                    s = term if s is None else s + term
                 parts.append(s)
             sums.append(jnp.concatenate(parts, axis=0))
         return sums[0] + shift_up(sums[1])
 
-    def put_plane(ref, z, rows):
-        ref[z] = jnp.concatenate([rows, shift_down(rows)], axis=0).astype(BF16)
-
-    def build_own(x_of):
-        for z in range(B):
-            put_plane(vb, z + 1, jnp.concatenate([x_of(z, d) for d in range(3)], axis=0))
-
-    def build_halo(p):
-        sides = rw[p, 0:2].reshape(96, half)
-        inner = jnp.concatenate([dot(t("put_y%d" % h), sides) for h in range(2)], axis=1)
-        ends = jnp.concatenate([dot(t("put_c%d" % b), rc[p]) for b in range(4)], axis=1)
-        for z in range(B):
-            put_plane(vh, z + 1, inner[8 * z : 8 * z + 8])
-        for k, z in enumerate((0, B + 1)):
-            put_plane(vh, z, ends[8 * k : 8 * k + 8])
-            put_plane(vb, z, joined(rw[p, 2 + k].astype(F32)))
+    def add_edges(p):
+        ends = []
+        for k in range(4):
+            v = rc[p, k].astype(F32)
+            ends.append(jnp.concatenate([v[8 * b : 8 * b + 8] for b in range(4)], axis=1))
+        sides = []
+        for side in range(2):
+            v = jnp.concatenate([joined(rw[p, side].astype(F32)), ends[side] + ends[side + 2]], axis=0)
+            sides += [v, shift_down(v)]
+        terms = dot(wside[...], jnp.concatenate(sides, axis=0).astype(BF16))
+        for side in range(2):
+            scales = [se[16 * side + 8 * cz : 16 * side + 8 * cz + 8] for cz in range(2)]
+            edge[side] = sums_of(terms[96 * side : 96 * side + 96], scales)
+        for side in range(2):
+            v = joined(rw[p, 2 + side].astype(F32))
+            v = jnp.concatenate([v, shift_down(v)], axis=0).astype(BF16)
+            none = jnp.zeros((96, nx), BF16)
+            first = 96 * (1 - side)
+            v = jnp.concatenate([none, v] if side else [v, none], axis=0)
+            terms = dot(wmat[first : first + 96, :144], v)
+            edge[2 + side] = sums_of(terms, [ss[B * side, 8 * cy : 8 * cy + 8] for cy in range(2)])
+
+    def apply(terms, scale_now, scale_below):
+        return sums_of(terms, [v[8 * cy : 8 * cy + 8] for v in (scale_now, scale_below) for cy in range(2)])
 
     def planes_of(own, edge, z, n):
         return jnp.concatenate([own[pl.ds(z, 3)].reshape(144, n), edge[pl.ds(z, 3)].reshape(48, n)], axis=0)
 
-    build_own(lambda z, d: start[d, z])
+    for z in range(B):
+        for d in range(3):
+            xs[z, 8 * d : 8 * d + 8] = start[d, z]
+    upd[...] = jnp.zeros_like(upd)
+    vb[0] = jnp.zeros((48, nx), BF16)
+    vb[B + 1] = jnp.zeros((48, nx), BF16)
     cs[...] = dot(picked[32:48].astype(BF16), t("pairs")).astype(BF16)
     cr[64:80] = cs[...]
 
@@ -419,7 +450,9 @@
 
     came = [joined(mr[m].astype(F32)) for m in range(3)]
     all_masks = jnp.concatenate([mask_wide] + came + [jnp.zeros((8, nx), F32)], axis=0).astype(BF16)
-    ss[...] = dot(t("mask_put"), all_masks).reshape(B + 1, 16, nx)
+    laid = dot(t("mask_put"), all_masks)
+    ss[...] = laid[0:144].reshape(B + 1, 16, nx)
+    se[...] = laid[144:176]
 
     def prepare(z, carry):
         for d in range(3):
@@ -448,41 +481,55 @@
 
     moves["load"].wait()
     moves["tab2"].wait()
-    for p in range(4):
-        if p > 0:
-            pack_field(p, [xs[z, 8 * d : 8 * d + 8] for z in range(B) for d in range(3)])
-            each(lambda k: field_copy(p, k), begin)
-            if p == 1:
-                each(scale_copy, begin)
-            build_own(lambda z, d: xs[z, 8 * d : 8 * d + 8])
+    row24 = lax.broadcasted_iota(jnp.int32, (24, nx), 0) % 8
+
+    def sweep(p, carry):
+        def pick(values):
+            v = jnp.float32(values[-1])
+            for i in range(len(values) - 2, -1, -1):
+                v = jnp.where(p == i, jnp.float32(values[i]), v)
+            return v
+
+        keep, gain = pick([0.0, steps[1][0], steps[2][0], 0.0]), pick([steps[0][1], steps[1][1], steps[2][1], 0.0])
+        for z in range(B):
+            put_plane(vb, z + 1, xs[z])
+        for z in range(B):
+            terms = dot(wmat[:, :144], vb[z : z + 3].reshape(144, nx))
+            res[z] = stack(load, z) - apply(terms, ss[z + 1], ss[z]) - three(idle[z]) * xs[z]
         arrived(lambda k: field_copy(p, k))
-        build_halo(p)
-
-        def plane(z):
-            x = stack(start, z) if p == 0 else xs[z]
-            kv = apply(planes_of(vb, vh, z, nx), ss[z + 1], ss[z])
-            r = stack(load, z) - kv - three(idle[z]) * x
-            if p < 3:
-                u = steps[p][1] * inv[z] * r
-                if p > 0:
-                    u = u + steps[p][0] * upd[z]
-                xs[z] = x + u
-                upd[z] = u
-            else:
-                upd[z] = r
-
-        def two(i, carry):
-            for j in range(4):
-                plane(4 * i + j)
-            return carry
-
-        lax.fori_loop(0, B // 4, two, 0)
+        add_edges(p)
+        for z in range(B):
+            sides = []
+            for side in range(2):
+                sides.append(jnp.concatenate([jnp.broadcast_to(edge[side, 8 * d + z : 8 * d + z + 1], (8, nx)) for d in range(3)], axis=0))
+            r = res[z] - jnp.where(row24 == 0, sides[0], jnp.where(row24 == 7, sides[1], 0.0))
+            if z == 0:
+                r = r - edge[2]
+            if z == B - 1:
+                r = r - edge[3]
+            u = gain * inv[z] * r + keep * upd[z]
+            res[z] = r
+            xs[z] = xs[z] + u
+            upd[z] = u
+
+        @pl.when(p < 3)
+        def _():
+            pack_field(p + 1, [xs[z, 8 * d : 8 * d + 8] for z in range(B) for d in range(3)])
+            each(lambda k: field_copy(p + 1, k), begin)
+
+        @pl.when(p == 0)
+        def _():
+            each(scale_copy, begin)
+
+        return carry
+
+    lax.fori_loop(0, 4, sweep, 0)
 
     def split(v):
         hi = v.astype(BF16)
         return hi, (v - hi.astype(F32)).astype(BF16)
 
-    hi, lo = split(upd[...].reshape(192, nx))
+    hi, lo = split(res[...].reshape(192, nx))
     narrow = dot(t("shrink"), hi) + dot(t("shrink"), lo)
     hi, lo = split(narrow)
     partial = dot(hi, t("down")) + dot(lo, t("down"))
@@ -536,7 +583,7 @@
 
     for p, (first, last) in ((1, (1, 7)), (2, (2, 6))):
         for k in range(first, last + 1):
-            kv = apply(planes_of(cvb, cvh, k - 1, half), css[k + 1], css[k])
+            kv = apply(dot(wmat[...], planes_of(cvb, cvh, k - 1, half)), css[k + 1], css[k])
             x = cx[k]
             r = crhs[k] - kv - three(cidle[k]) * x
             u = steps[p][0] * cu[k] + steps[p][1] * cinv[k, 0:24] * r
@@ -585,13 +632,15 @@
             pltpu.VMEM((B, 24, nx), F32),
             pltpu.VMEM((B, 24, nx), F32),
             pltpu.VMEM((B, 8, nx), F32),
+            pltpu.VMEM((B, 24, nx), F32),
+            pltpu.VMEM((4, 24, nx), F32),
             pltpu.VMEM((B + 1, 16, nx), F32),
+            pltpu.VMEM((32, nx), F32),
             pltpu.VMEM((B + 2, 48, nx), BF16),
-            pltpu.VMEM((B + 2, 16, nx), BF16),
             pltpu.VMEM((4, 4, 48, half), BF16),
-            pltpu.VMEM((4, 64, quarter), BF16),
+            pltpu.VMEM((4, 4, 32, quarter), BF16),
             pltpu.VMEM((4, 4, 48, half), BF16),
-            pltpu.VMEM((4, 64, quarter), BF16),
+            pltpu.VMEM((4, 4, 32, quarter), BF16),
             pltpu.VMEM((3, 16, half), BF16),
             pltpu.VMEM((3, 16, half), BF16),
             pltpu.VMEM((16, half), BF16),
@@ -607,9 +656,10 @@
             pltpu.VMEM((9, 48, half), BF16),
             pltpu.VMEM((9, 16, half), BF16),
             pltpu.VMEM((192, 192), BF16),
+            pltpu.VMEM((192, 128), BF16),
             dma((7,)), dma((4, 8)), dma((4, 8)), dma((3,)), dma((3,)), dma((8,)), dma((8,)), dma((8,)), dma((8,)),
         ],
-        compiler_params=pltpu.CompilerParams(collective_id=0, has_side_effects=True, vmem_limit_bytes=48 * 1024 * 1024),
+        compiler_params=pltpu.CompilerParams(collective_id=0, has_side_effects=True, vmem_limit_bytes=62 * 1024 * 1024),
     )(*given)
 
 

time: 38.8 us -> 29.8 us (0.77)
  local copies, waits for them, and re-layouts: 7.78 us -> 1.77 us
  Pallas kernels: 30.6 us -> 27.9 us
    unnamed x15 -> x1, local copies, waits for them, and re-layouts: 7.78 us -> 1.77 us
    pallas_call x1, Pallas kernels: 30.6 us -> 27.9 us  [body(): pl.pallas_call(functools.partial(kernel, where, n_z, n_y), out_shape=jax....]
where the time goes in v2:
time: 29.8 us; the launch traced here: 29.7 us
  Pallas kernels  27.9 us (94%)
  local copies, waits for them, and re-layouts  1.77 us (6%)
    pallas_call x1, Pallas kernels, body(): pl.pallas_call(functools.partial(kernel, where, n_z, n_y), out_shape=jax....  27.9 us
    unnamed x1, local copies, waits for them, and re-layouts  1.77 us

profile of v2, /device:TPU:3, one launch (start us, length us, event | category | flops | bytes accessed | tf_op | source)
XLA Modules:
  0.0 29.7 jit_solution(5671759025012434179)
XLA Ops:
  0.0 27.9 %shard_map.73 = f32[3,8,8,512]{3,2,1,0:T(8,128)} custom-call(f32[3,8,8,512]{3,2,1,0:T(8,128)} %load_h.1, f32[3,8,8,512]{3,2,1,0:T(8,128)} %start_h.1, s32[8,8,512]{2,1,0:T(8,128)} %mask_h.1, bf16[24,24]{1,0:T(8,128)(2,1)} %stiff_h.1, bf16[128,256]{1,0:T(8,128)(2,1)} %constant.6.clone.tab0_h, bf16[3904,256]{1,0:T(8,128)(2,1)} %constant.7.clone.tab1_h, ...), custom_call_target="tpu_custom_call" | custom-call | tf_op jit(solution)/shard_map/pallas_call | solution.py:624
  27.9 1.8 %copy.9 = f32[3,8,8,512]{3,2,1,0:T(8,128)} copy(f32[3,8,8,512]{3,2,1,0:T(8,128)} %shard_map.73) | data formatting | bytes 786432

commit v3 on v2

--- a/solution.py
+++ b/solution.py
@@ -69,7 +69,8 @@
             sel[24 + z * 3 + d, z * 24 + d * 8 + 7] = 1
         for k, (dz, dy) in enumerate(NEAR[:4]):
             z, y = 7 if dz > 0 else 0, 7 if dy > 0 else 0
-            sel[48 + 8 * k + (0 if dz > 0 else 3) + d, z * 24 + d * 8 + y] = 1
+            sel[48 + 8 * k + d, z * 24 + d * 8 + y] = 1
+            sel[52 + 8 * k + d, z * 24 + d * 8 + y] = 1
     out["sel"] = sel
     rep_y = np.zeros((192, EDOF))
     rows_y = []
@@ -83,10 +84,10 @@
         keep = np.zeros((192, 128))
         for col in range(128):
             side, sx, rc = col // 64, col // 32 % 2, col % 32
-            if rc >= 30:
+            if rc >= 24 and rc % 4 == 3:
                 continue
-            z2 = rc // 3 if rc < 24 else (-1 if rc < 27 else 8)
-            pick[3 * (4 * cz2 + 2 * side + sx) + rc % 3, col] = 1
+            z2, d = (rc // 3, rc % 3) if rc < 24 else (-1 if rc < 28 else 8, rc % 4)
+            pick[3 * (4 * cz2 + 2 * side + sx) + d, col] = 1
             for r, (row_side, cz, z) in enumerate(rows_y):
                 if row_side == side and z2 == z - cz + cz2:
                     keep[r, col] = 1
@@ -164,7 +165,7 @@
                         grow[z * 24 + d * 8 + y, k * 24 + d * 8 + j + 1] = w
     out["shrink"], out["grow"] = shrink, grow
     hand = np.zeros((RHS_ALL, 80))
-    gather = np.zeros((288, RHS_ALL + 160))
+    gather = np.zeros((288, RHS_ALL + 80))
 
     def message(dz, dy):
         (z0, nz), (y0, ny) = EDGE[dz], EDGE[dy]
@@ -183,8 +184,7 @@
             if -2 <= k2 <= 6 and y2 == -2:
                 gather[(k2 + 2) * 32 + 24 + d, at + i] = 1
     for (k, y, d), i in own.items():
-        for at in (RHS_ALL, RHS_ALL + 80):
-            gather[(k + 2) * 32 + d * 8 + y + 1, at + i] = 1
+        gather[(k + 2) * 32 + d * 8 + y + 1, RHS_ALL + i] = 1
     out["hand"], out["gather"] = hand, gather
     return out
 
@@ -213,9 +213,9 @@
     return where, packed
 
 
-def kernel(where, n_z, n_y, load_h, start_h, mask_h, stiff_h, tab0_h, tab1_h, tab2_h, out, load, start, mask, stiff, tab0, tab1, tab2,
+def kernel(where, n_z, n_y, load_h, start_h, mask_h, stiff_h, tab0_h, tab1_h, tab2_h, smooth_h, fix_h, load, start, mask, stiff, tab0, tab1, tab2,
            xs, upd, inv, idle, res, edge, ss, se, vb, sw, sc, rw, rc, mr, ms, cs, cr, rsend_buf, rr, cx, cu, cinv, cidle, css, crhs, cvb, cvh,
-           wmat, wside, local_sem, send_sem, recv_sem, msend, mrecv, csend, crecv, rsend, rrecv):
+           wmat, wside, local_sem, out_sem, send_sem, recv_sem, msend, mrecv, csend, crecv, rsend, rrecv):
     nx = load.shape[-1]
     half, quarter = nx // 2, nx // 4
     gz, gy = lax.axis_index("gz"), lax.axis_index("gy")
@@ -256,7 +256,7 @@
         @pl.when(jnp.logical_not(exists(dz, dy)))
         def _():
             if k < 4:
-                rc[:, k] = jnp.zeros((4, 32, quarter), BF16)
+                rc[:, k] = jnp.zeros((4, 16, quarter), BF16)
             else:
                 rw[:, k - 4] = jnp.zeros((4, 48, half), BF16)
             slot = ((dz + 1) * 3 + dy + 1) * 16
@@ -300,12 +300,15 @@
         n = v.shape[0] // 2
         return jnp.concatenate([v[:n], v[n:]], axis=1)
 
+    low4 = lax.broadcasted_iota(jnp.int32, (8, quarter), 0) < 4
+
     def pack_field(p, planes):
         own = jnp.concatenate(planes, axis=0).astype(BF16)
         rows = dot(t("sel"), own)
         for k in range(4):
             v = rows[48 + 8 * k : 56 + 8 * k]
-            sc[p, k] = jnp.concatenate([v[:, b * quarter : (b + 1) * quarter] for b in range(4)], axis=0).astype(BF16)
+            v = [v[:, b * quarter : (b + 1) * quarter] for b in range(4)]
+            sc[p, k] = jnp.concatenate([jnp.where(low4, v[0], v[1]), jnp.where(low4, v[2], v[3])], axis=0).astype(BF16)
         sw[p, 0] = halves(rows[0:24]).astype(BF16)
         sw[p, 1] = halves(rows[24:48]).astype(BF16)
         sw[p, 2] = halves(jnp.concatenate(planes[0:3], axis=0)).astype(BF16)
@@ -407,12 +410,19 @@
 
     def add_edges(p):
         ends = []
-        for k in range(4):
-            v = rc[p, k].astype(F32)
-            ends.append(jnp.concatenate([v[8 * b : 8 * b + 8] for b in range(4)], axis=1))
+        for side in range(2):
+            near, far = rc[p, side].astype(F32), rc[p, side + 2].astype(F32)
+            blocks = []
+            for b in range(4):
+                rows = slice(8 * (b // 2), 8 * (b // 2) + 8)
+                if b % 2:
+                    blocks.append(jnp.where(low4, pltpu.roll(near[rows], 4, axis=0), far[rows]))
+                else:
+                    blocks.append(jnp.where(low4, near[rows], pltpu.roll(far[rows], 4, axis=0)))
+            ends.append(jnp.concatenate(blocks, axis=1))
         sides = []
         for side in range(2):
-            v = jnp.concatenate([joined(rw[p, side].astype(F32)), ends[side] + ends[side + 2]], axis=0)
+            v = jnp.concatenate([joined(rw[p, side].astype(F32)), ends[side]], axis=0)
             sides += [v, shift_down(v)]
         terms = dot(wside[...], jnp.concatenate(sides, axis=0).astype(BF16))
         for side in range(2):
@@ -525,19 +535,14 @@
 
     lax.fori_loop(0, 4, sweep, 0)
 
-    def split(v):
-        hi = v.astype(BF16)
-        return hi, (v - hi.astype(F32)).astype(BF16)
-
-    hi, lo = split(res[...].reshape(192, nx))
-    narrow = dot(t("shrink"), hi) + dot(t("shrink"), lo)
-    hi, lo = split(narrow)
-    partial = dot(hi, t("down")) + dot(lo, t("down"))
-    hi, lo = split(partial)
+    for d in range(3):
+        pltpu.make_async_copy(xs.at[:, 8 * d : 8 * d + 8], smooth_h.at[d], out_sem.at[d]).start()
+
+    narrow = dot(t("shrink"), res[...].reshape(192, nx).astype(BF16))
+    hi = dot(narrow.astype(BF16), t("down")).astype(BF16)
     rsend_buf[...] = dot(t("hand"), hi).astype(BF16)
     each(rhs_copy, begin)
     rr[RHS_ALL : RHS_ALL + 80] = hi
-    rr[RHS_ALL + 80 : RHS_ALL + 160] = lo
 
     arrived(scale_copy)
     css[...] = dot(t("cs_put"), cr[...]).reshape(10, 32, half)
@@ -595,12 +600,10 @@
                 cvh[k] = jnp.zeros((16, half), BF16)
 
     fix = cx[2:7].reshape(120, half).astype(BF16)
-    hi, lo = split(dot(t("grow"), fix))
-    side = dot(hi, t("up")) + dot(lo, t("up"))
-    for z in range(B):
-        for d in range(3):
-            at = z * 24 + d * 8
-            out[d, z] = xs[z, 8 * d : 8 * d + 8] + side[at : at + 8]
+    side = dot(dot(t("grow"), fix).astype(BF16), t("up"))
+    res[...] = side.reshape(B, 24, nx)
+    for d in range(3):
+        pltpu.make_async_copy(res.at[:, 8 * d : 8 * d + 8], fix_h.at[d], out_sem.at[3 + d]).start()
 
     for p in range(4):
         each(lambda k: field_copy(p, k), lambda c: c.wait_send())
@@ -611,6 +614,9 @@
         @pl.when(exists(*mask_to[m]))
         def _():
             mask_copy(m).wait_send()
+    for d in range(3):
+        pltpu.make_async_copy(xs.at[:, 8 * d : 8 * d + 8], smooth_h.at[d], out_sem.at[d]).wait()
+        pltpu.make_async_copy(res.at[:, 8 * d : 8 * d + 8], fix_h.at[d], out_sem.at[3 + d]).wait()
 
 
 def body(n_z, n_y, load, start, mask, stiff):
@@ -619,13 +625,12 @@
     where, packed = pack_tables(nx)
     given = [load, start, mask, stiff] + [jnp.asarray(v) for v in packed]
     dma = pltpu.SemaphoreType.DMA
-    vmem = pl.BlockSpec(memory_space=pltpu.VMEM)
     hbm = pl.BlockSpec(memory_space=pltpu.HBM)
-    return pl.pallas_call(
+    smooth, fix = pl.pallas_call(
         functools.partial(kernel, where, n_z, n_y),
-        out_shape=jax.ShapeDtypeStruct(load.shape, F32),
+        out_shape=[jax.ShapeDtypeStruct(load.shape, F32)] * 2,
         in_specs=[hbm] * len(given),
-        out_specs=vmem,
+        out_specs=[hbm] * 2,
         scratch_shapes=[pltpu.VMEM(v.shape, v.dtype) for v in given]
         + [
             pltpu.VMEM((B, 24, nx), F32),
@@ -638,15 +643,15 @@
             pltpu.VMEM((32, nx), F32),
             pltpu.VMEM((B + 2, 48, nx), BF16),
             pltpu.VMEM((4, 4, 48, half), BF16),
-            pltpu.VMEM((4, 4, 32, quarter), BF16),
+            pltpu.VMEM((4, 4, 16, quarter), BF16),
             pltpu.VMEM((4, 4, 48, half), BF16),
-            pltpu.VMEM((4, 4, 32, quarter), BF16),
+            pltpu.VMEM((4, 4, 16, quarter), BF16),
             pltpu.VMEM((3, 16, half), BF16),
             pltpu.VMEM((3, 16, half), BF16),
             pltpu.VMEM((16, half), BF16),
             pltpu.VMEM((144, half), BF16),
             pltpu.VMEM((RHS_ALL, half), BF16),
-            pltpu.VMEM((RHS_ALL + 160, half), BF16),
+            pltpu.VMEM((RHS_ALL + 80, half), BF16),
             pltpu.VMEM((9, 24, half), F32),
             pltpu.VMEM((9, 24, half), F32),
             pltpu.VMEM((9, 32, half), F32),
@@ -657,10 +662,11 @@
             pltpu.VMEM((9, 16, half), BF16),
             pltpu.VMEM((192, 192), BF16),
             pltpu.VMEM((192, 128), BF16),
-            dma((7,)), dma((4, 8)), dma((4, 8)), dma((3,)), dma((3,)), dma((8,)), dma((8,)), dma((8,)), dma((8,)),
+            dma((7,)), dma((6,)), dma((4, 8)), dma((4, 8)), dma((3,)), dma((3,)), dma((8,)), dma((8,)), dma((8,)), dma((8,)),
         ],
         compiler_params=pltpu.CompilerParams(collective_id=0, has_side_effects=True, vmem_limit_bytes=62 * 1024 * 1024),
     )(*given)
+    return smooth + fix
 
 
 def solution(mesh):

time: 29.8 us -> 29.5 us (0.990)
  other arithmetic: 0 us -> 1.92 us
  local copies, waits for them, and re-layouts: 1.77 us -> 0 us
  Pallas kernels: 27.9 us -> 27.4 us
    add x0 -> x1, other arithmetic: none -> 1.92 us  [body(): return smooth + fix]
    unnamed x1 -> x0, local copies, waits for them, and re-layouts: 1.77 us -> none
    pallas_call x1, Pallas kernels: 27.9 us -> 27.4 us  [body(): pl.pallas_call(functools.partial(kernel, where, n_z, n_y), out_shape=[jax...]
where the time goes in v3:
time: 29.5 us; the launch traced here: 29.4 us
  Pallas kernels  27.4 us (93%)
  other arithmetic  1.92 us (7%)
    pallas_call x1, Pallas kernels, body(): pl.pallas_call(functools.partial(kernel, where, n_z, n_y), out_shape=[jax...  27.4 us
    add x1, other arithmetic, body(): return smooth + fix  1.92 us

profile of v3, /device:TPU:3, one launch (start us, length us, event | category | flops | bytes accessed | tf_op | source)
XLA Modules:
  0.0 29.4 jit_solution(13702343487543060660)
XLA Ops:
  0.0 27.4 %shard_map.73 = (f32[3,8,8,512]{3,2,1,0:T(8,128)}, f32[3,8,8,512]{3,2,1,0:T(8,128)}) custom-call(f32[3,8,8,512]{3,2,1,0:T(8,128)} %load_h.1, f32[3,8,8,512]{3,2,1,0:T(8,128)} %start_h.1, s32[8,8,512]{2,1,0:T(8,128)} %mask_h.1, bf16[24,24]{1,0:T(8,128)(2,1)} %stiff_h.1, bf16[128,256]{1,0:T(8,128)(2,1)} %constant.6.clone.tab0_h, ...), custom_call_target="tpu_custom_call" | custom-call | tf_op jit(solution)/shard_map/pallas_call | solution.py:629
  27.4 1.9 %add.3 = f32[3,8,8,512]{3,2,1,0:T(8,128)} add(f32[3,8,8,512]{3,2,1,0:T(8,128)} %get-tuple-element.7, f32[3,8,8,512]{3,2,1,0:T(8,128)} %get-tuple-element.8) | non-fusion elementwise | flops 98304 | bytes 1179648 | tf_op jit(solution)/shard_map/add | solution.py:669

commit v4 on v3

--- a/solution.py
+++ b/solution.py
@@ -62,16 +62,6 @@
                         keep[r, col] = 1
             out["pick%d%d" % (cz2, cy2)] = pick
             out["keep%d%d" % (cz2, cy2)] = keep
-    sel = np.zeros((80, 192))
-    for d in range(3):
-        for z in range(B):
-            sel[z * 3 + d, z * 24 + d * 8] = 1
-            sel[24 + z * 3 + d, z * 24 + d * 8 + 7] = 1
-        for k, (dz, dy) in enumerate(NEAR[:4]):
-            z, y = 7 if dz > 0 else 0, 7 if dy > 0 else 0
-            sel[48 + 8 * k + d, z * 24 + d * 8 + y] = 1
-            sel[52 + 8 * k + d, z * 24 + d * 8 + y] = 1
-    out["sel"] = sel
     rep_y = np.zeros((192, EDOF))
     rows_y = []
     for r in range(192):
@@ -86,7 +76,7 @@
             side, sx, rc = col // 64, col // 32 % 2, col % 32
             if rc >= 24 and rc % 4 == 3:
                 continue
-            z2, d = (rc // 3, rc % 3) if rc < 24 else (-1 if rc < 28 else 8, rc % 4)
+            z2, d = (rc % 8, rc // 8) if rc < 24 else (-1 if rc < 28 else 8, rc % 4)
             pick[3 * (4 * cz2 + 2 * side + sx) + d, col] = 1
             for r, (row_side, cz, z) in enumerate(rows_y):
                 if row_side == side and z2 == z - cz + cz2:
@@ -189,7 +179,7 @@
     return out
 
 
-EARLY = ["sel", "mask_sel"]
+EARLY = ["mask_sel"]
 
 
 def pack_tables(nx):
@@ -302,17 +292,30 @@
 
     low4 = lax.broadcasted_iota(jnp.int32, (8, quarter), 0) < 4
 
-    def pack_field(p, planes):
-        own = jnp.concatenate(planes, axis=0).astype(BF16)
-        rows = dot(t("sel"), own)
+    row8 = lax.broadcasted_iota(jnp.int32, (8, nx), 0)
+
+    def spread(row):
+        return jnp.broadcast_to(row, (8, nx))
+
+    def pack_field(p):
+        for side, y in enumerate((0, 7)):
+            rows = []
+            for d in range(3):
+                v = spread(xs[0, 8 * d + y : 8 * d + y + 1])
+                for z in range(1, B):
+                    v = jnp.where(row8 == z, spread(xs[z, 8 * d + y : 8 * d + y + 1]), v)
+                rows.append(v)
+            sw[p, side] = halves(jnp.concatenate(rows, axis=0)).astype(BF16)
         for k in range(4):
-            v = rows[48 + 8 * k : 56 + 8 * k]
+            z, y = 7 if NEAR[k][0] > 0 else 0, 7 if NEAR[k][1] > 0 else 0
+            v = spread(xs[z, y : y + 1])
+            for d in (1, 2):
+                v = jnp.where(row8 % 4 == d, spread(xs[z, 8 * d + y : 8 * d + y + 1]), v)
+            v = jnp.where(row8 % 4 == 3, 0.0, v)
             v = [v[:, b * quarter : (b + 1) * quarter] for b in range(4)]
             sc[p, k] = jnp.concatenate([jnp.where(low4, v[0], v[1]), jnp.where(low4, v[2], v[3])], axis=0).astype(BF16)
-        sw[p, 0] = halves(rows[0:24]).astype(BF16)
-        sw[p, 1] = halves(rows[24:48]).astype(BF16)
-        sw[p, 2] = halves(jnp.concatenate(planes[0:3], axis=0)).astype(BF16)
-        sw[p, 3] = halves(jnp.concatenate(planes[21:24], axis=0)).astype(BF16)
+        sw[p, 2] = halves(xs[0]).astype(BF16)
+        sw[p, 3] = halves(xs[B - 1]).astype(BF16)
 
     def each(copy, do, ks=range(8)):
         for k in ks:
@@ -328,8 +331,11 @@
         each(lambda k: copy(back(k)), lambda c: c.wait_recv())
 
     moves["start"].wait()
+    for z in range(B):
+        for d in range(3):
+            xs[z, 8 * d : 8 * d + 8] = start[d, z]
+    pack_field(0)
     moves["tab0"].wait()
-    pack_field(0, [start[d, z] for z in range(B) for d in range(3)])
     moves["mask"].wait()
     mask_wide = jnp.concatenate([mask[z] for z in range(B)], axis=0).astype(F32)
     picked = dot(t("mask_sel"), mask_wide.astype(BF16))
@@ -443,9 +449,6 @@
     def planes_of(own, edge, z, n):
         return jnp.concatenate([own[pl.ds(z, 3)].reshape(144, n), edge[pl.ds(z, 3)].reshape(48, n)], axis=0)
 
-    for z in range(B):
-        for d in range(3):
-            xs[z, 8 * d : 8 * d + 8] = start[d, z]
     upd[...] = jnp.zeros_like(upd)
     vb[0] = jnp.zeros((48, nx), BF16)
     vb[B + 1] = jnp.zeros((48, nx), BF16)
@@ -464,16 +467,13 @@
     ss[...] = laid[0:144].reshape(B + 1, 16, nx)
     se[...] = laid[144:176]
 
-    def prepare(z, carry):
+    for z in range(B):
         for d in range(3):
             dg = diagonal(lambda layer, cy: ss[layer + 1, cy * 8 : cy * 8 + 8], z, d)
             no = jnp.where(dg == 0.0, 1.0, 0.0)
             inv[z, d * 8 : d * 8 + 8] = 1.0 / ((dg + no) * bound)
             if d == 0:
                 idle[z] = no
-        return carry
-
-    lax.fori_loop(0, B, prepare, 0)
 
     ratio = (1.0 + LOW) / (1.0 - LOW)
     rho = [1.0 / ratio]
@@ -524,7 +524,7 @@
 
         @pl.when(p < 3)
         def _():
-            pack_field(p + 1, [xs[z, 8 * d : 8 * d + 8] for z in range(B) for d in range(3)])
+            pack_field(p + 1)
             each(lambda k: field_copy(p + 1, k), begin)
 
         @pl.when(p == 0)
@@ -547,8 +547,7 @@
     arrived(scale_copy)
     css[...] = dot(t("cs_put"), cr[...]).reshape(10, 32, half)
     last_z, last_y = gz == n_z - 1, gy == n_y - 1
-    row8 = lax.broadcasted_iota(jnp.int32, (8, half), 0)
-    good_y = jnp.where(jnp.logical_and(last_y, row8 >= C + 1), 0.0, 1.0)
+    good_y = jnp.where(jnp.logical_and(last_y, row8[:, :half] >= C + 1), 0.0, 1.0)
     for k in range(9):
         good = good_y
         if k - 2 >= C:

time: 29.5 us -> 28.6 us (0.969)
  Pallas kernels: 27.4 us -> 26.5 us
    pallas_call x1, Pallas kernels: 27.4 us -> 26.5 us  [body(): pl.pallas_call(functools.partial(kernel, where, n_z, n_y), out_shape=[jax...]
where the time goes in v4:
time: 28.6 us; the launch traced here: 28.4 us
  Pallas kernels  26.5 us (93%)
  other arithmetic  1.92 us (7%)
    pallas_call x1, Pallas kernels, body(): pl.pallas_call(functools.partial(kernel, where, n_z, n_y), out_shape=[jax...  26.5 us
    add x1, other arithmetic, body(): return smooth + fix  1.92 us

profile of v4, /device:TPU:3, one launch (start us, length us, event | category | flops | bytes accessed | tf_op | source)
XLA Modules:
  0.0 28.4 jit_solution(2770533594467249016)
XLA Ops:
  0.0 26.5 %shard_map.73 = (f32[3,8,8,512]{3,2,1,0:T(8,128)}, f32[3,8,8,512]{3,2,1,0:T(8,128)}) custom-call(f32[3,8,8,512]{3,2,1,0:T(8,128)} %load_h.1, f32[3,8,8,512]{3,2,1,0:T(8,128)} %start_h.1, s32[8,8,512]{2,1,0:T(8,128)} %mask_h.1, bf16[24,24]{1,0:T(8,128)(2,1)} %stiff_h.1, bf16[48,128]{1,0:T(8,128)(2,1)} %constant.6.clone.tab0_h, ...), custom_call_target="tpu_custom_call" | custom-call | tf_op jit(solution)/shard_map/pallas_call | solution.py:628
  26.5 1.9 %add.3 = f32[3,8,8,512]{3,2,1,0:T(8,128)} add(f32[3,8,8,512]{3,2,1,0:T(8,128)} %get-tuple-element.7, f32[3,8,8,512]{3,2,1,0:T(8,128)} %get-tuple-element.8) | non-fusion elementwise | flops 98304 | bytes 1179648 | tf_op jit(solution)/shard_map/add | solution.py:668

commit v5 on v4

--- a/solution.py
+++ b/solution.py
@@ -204,7 +204,7 @@
 
 
 def kernel(where, n_z, n_y, load_h, start_h, mask_h, stiff_h, tab0_h, tab1_h, tab2_h, smooth_h, fix_h, load, start, mask, stiff, tab0, tab1, tab2,
-           xs, upd, inv, idle, res, edge, ss, se, vb, sw, sc, rw, rc, mr, ms, cs, cr, rsend_buf, rr, cx, cu, cinv, cidle, css, crhs, cvb, cvh,
+           xs, upd, inv, idle, res, edge, ss, se, vb, sw, sc, rw, rc, mr, ms, pk, cs, cr, rsend_buf, rr, cx, cu, cinv, cidle, css, crhs, cvb, cvh,
            wmat, wside, local_sem, out_sem, send_sem, recv_sem, msend, mrecv, csend, crecv, rsend, rrecv):
     nx = load.shape[-1]
     half, quarter = nx // 2, nx // 4
@@ -330,6 +330,9 @@
     def arrived(copy):
         each(lambda k: copy(back(k)), lambda c: c.wait_recv())
 
+    upd[...] = jnp.zeros_like(upd)
+    vb[0] = jnp.zeros((48, nx), BF16)
+    vb[B + 1] = jnp.zeros((48, nx), BF16)
     moves["start"].wait()
     for z in range(B):
         for d in range(3):
@@ -339,6 +342,7 @@
     moves["mask"].wait()
     mask_wide = jnp.concatenate([mask[z] for z in range(B)], axis=0).astype(F32)
     picked = dot(t("mask_sel"), mask_wide.astype(BF16))
+    pk[...] = picked[32:48].astype(BF16)
     for m in range(3):
         ms[m] = halves(picked[8 * m : 8 * m + 8]).astype(BF16)
 
@@ -400,19 +404,24 @@
     def put_plane(ref, z, rows):
         ref[z] = jnp.concatenate([rows, shift_down(rows)], axis=0).astype(BF16)
 
-    def sums_of(terms, scales):
-        sums = []
-        for c in range(2):
-            parts = []
-            for d in range(3):
-                s = None
-                for g, sc_g in enumerate(scales):
-                    at = (2 * g + c) * 24 + d * 8
-                    term = terms[at : at + 8] * sc_g
-                    s = term if s is None else s + term
-                parts.append(s)
-            sums.append(jnp.concatenate(parts, axis=0))
-        return sums[0] + shift_up(sums[1])
+    def sums_of(matrix, planes, scales):
+        n = planes.shape[1]
+        sums = [[], []]
+        for first in range(0, n, 256):
+            lanes = slice(first, min(first + 256, n))
+            terms = dot(matrix, planes[:, lanes])
+            for c in range(2):
+                parts = []
+                for d in range(3):
+                    s = None
+                    for g, sc_g in enumerate(scales):
+                        at = (2 * g + c) * 24 + d * 8
+                        term = terms[at : at + 8] * sc_g[:, lanes]
+                        s = term if s is None else s + term
+                    parts.append(s)
+                sums[c].append(jnp.concatenate(parts, axis=0))
+        low, high = [jnp.concatenate(v, axis=1) if len(v) > 1 else v[0] for v in sums]
+        return low + shift_up(high)
 
     def add_edges(p):
         ends = []
@@ -430,30 +439,24 @@
         for side in range(2):
             v = jnp.concatenate([joined(rw[p, side].astype(F32)), ends[side]], axis=0)
             sides += [v, shift_down(v)]
-        terms = dot(wside[...], jnp.concatenate(sides, axis=0).astype(BF16))
+        sides = jnp.concatenate(sides, axis=0).astype(BF16)
         for side in range(2):
             scales = [se[16 * side + 8 * cz : 16 * side + 8 * cz + 8] for cz in range(2)]
-            edge[side] = sums_of(terms[96 * side : 96 * side + 96], scales)
+            edge[side] = sums_of(wside[96 * side : 96 * side + 96], sides, scales)
         for side in range(2):
             v = joined(rw[p, 2 + side].astype(F32))
             v = jnp.concatenate([v, shift_down(v)], axis=0).astype(BF16)
             none = jnp.zeros((96, nx), BF16)
             first = 96 * (1 - side)
             v = jnp.concatenate([none, v] if side else [v, none], axis=0)
-            terms = dot(wmat[first : first + 96, :144], v)
-            edge[2 + side] = sums_of(terms, [ss[B * side, 8 * cy : 8 * cy + 8] for cy in range(2)])
-
-    def apply(terms, scale_now, scale_below):
-        return sums_of(terms, [v[8 * cy : 8 * cy + 8] for v in (scale_now, scale_below) for cy in range(2)])
+            edge[2 + side] = sums_of(wmat[first : first + 96, :144], v, [ss[B * side, 8 * cy : 8 * cy + 8] for cy in range(2)])
+
+    def apply(matrix, planes, scale_now, scale_below):
+        return sums_of(matrix, planes, [v[8 * cy : 8 * cy + 8] for v in (scale_now, scale_below) for cy in range(2)])
 
     def planes_of(own, edge, z, n):
         return jnp.concatenate([own[pl.ds(z, 3)].reshape(144, n), edge[pl.ds(z, 3)].reshape(48, n)], axis=0)
 
-    upd[...] = jnp.zeros_like(upd)
-    vb[0] = jnp.zeros((48, nx), BF16)
-    vb[B + 1] = jnp.zeros((48, nx), BF16)
-    cs[...] = dot(picked[32:48].astype(BF16), t("pairs")).astype(BF16)
-    cr[64:80] = cs[...]
 
     for m in range(3):
 
@@ -504,8 +507,8 @@
         for z in range(B):
             put_plane(vb, z + 1, xs[z])
         for z in range(B):
-            terms = dot(wmat[:, :144], vb[z : z + 3].reshape(144, nx))
-            res[z] = stack(load, z) - apply(terms, ss[z + 1], ss[z]) - three(idle[z]) * xs[z]
+            planes = vb[z : z + 3].reshape(144, nx)
+            res[z] = stack(load, z) - apply(wmat[:, :144], planes, ss[z + 1], ss[z]) - three(idle[z]) * xs[z]
         arrived(lambda k: field_copy(p, k))
         add_edges(p)
         for z in range(B):
@@ -529,6 +532,8 @@
 
         @pl.when(p == 0)
         def _():
+            cs[...] = dot(pk[...], t("pairs")).astype(BF16)
+            cr[64:80] = cs[...]
             each(scale_copy, begin)
 
         return carry
@@ -587,7 +592,7 @@
 
     for p, (first, last) in ((1, (1, 7)), (2, (2, 6))):
         for k in range(first, last + 1):
-            kv = apply(dot(wmat[...], planes_of(cvb, cvh, k - 1, half)), css[k + 1], css[k])
+            kv = apply(wmat[...], planes_of(cvb, cvh, k - 1, half), css[k + 1], css[k])
             x = cx[k]
             r = crhs[k] - kv - three(cidle[k]) * x
             u = steps[p][0] * cu[k] + steps[p][1] * cinv[k, 0:24] * r
@@ -599,10 +604,16 @@
                 cvh[k] = jnp.zeros((16, half), BF16)
 
     fix = cx[2:7].reshape(120, half).astype(BF16)
-    side = dot(dot(t("grow"), fix).astype(BF16), t("up"))
-    res[...] = side.reshape(B, 24, nx)
-    for d in range(3):
-        pltpu.make_async_copy(res.at[:, 8 * d : 8 * d + 8], fix_h.at[d], out_sem.at[3 + d]).start()
+    grown = dot(t("grow"), fix).astype(BF16)
+
+    def fix_copy(part, d):
+        at = C * part
+        return pltpu.make_async_copy(res.at[at : at + C, 8 * d : 8 * d + 8], fix_h.at[d, at : at + C], out_sem.at[3 + 3 * part + d])
+
+    for part in range(2):
+        res[C * part : C * part + C] = dot(grown[96 * part : 96 * part + 96], t("up")).reshape(C, 24, nx)
+        for d in range(3):
+            fix_copy(part, d).start()
 
     for p in range(4):
         each(lambda k: field_copy(p, k), lambda c: c.wait_send())
@@ -615,7 +626,8 @@
             mask_copy(m).wait_send()
     for d in range(3):
         pltpu.make_async_copy(xs.at[:, 8 * d : 8 * d + 8], smooth_h.at[d], out_sem.at[d]).wait()
-        pltpu.make_async_copy(res.at[:, 8 * d : 8 * d + 8], fix_h.at[d], out_sem.at[3 + d]).wait()
+        for part in range(2):
+            fix_copy(part, d).wait()
 
 
 def body(n_z, n_y, load, start, mask, stiff):
@@ -647,6 +659,7 @@
             pltpu.VMEM((4, 4, 16, quarter), BF16),
             pltpu.VMEM((3, 16, half), BF16),
             pltpu.VMEM((3, 16, half), BF16),
+            pltpu.VMEM((16, nx), BF16),
             pltpu.VMEM((16, half), BF16),
             pltpu.VMEM((144, half), BF16),
             pltpu.VMEM((RHS_ALL, half), BF16),
@@ -661,7 +674,7 @@
             pltpu.VMEM((9, 16, half), BF16),
             pltpu.VMEM((192, 192), BF16),
             pltpu.VMEM((192, 128), BF16),
-            dma((7,)), dma((6,)), dma((4, 8)), dma((4, 8)), dma((3,)), dma((3,)), dma((8,)), dma((8,)), dma((8,)), dma((8,)),
+            dma((7,)), dma((9,)), dma((4, 8)), dma((4, 8)), dma((3,)), dma((3,)), dma((8,)), dma((8,)), dma((8,)), dma((8,)),
         ],
         compiler_params=pltpu.CompilerParams(collective_id=0, has_side_effects=True, vmem_limit_bytes=62 * 1024 * 1024),
     )(*given)

time: 28.6 us -> 28.6 us (level)
  no operation moved by 1% of the time
where the time goes in v5:
time: 28.6 us; the launch traced here: 28.4 us
  Pallas kernels  26.5 us (93%)
  other arithmetic  1.92 us (7%)
    pallas_call x1, Pallas kernels, body(): pl.pallas_call(functools.partial(kernel, where, n_z, n_y), out_shape=[jax...  26.5 us
    add x1, other arithmetic, body(): return smooth + fix  1.92 us

profile of v5, /device:TPU:3, one launch (start us, length us, event | category | flops | bytes accessed | tf_op | source)
XLA Modules:
  0.0 28.4 jit_solution(17865542920106001138)
XLA Ops:
  0.0 26.5 %shard_map.73 = (f32[3,8,8,512]{3,2,1,0:T(8,128)}, f32[3,8,8,512]{3,2,1,0:T(8,128)}) custom-call(f32[3,8,8,512]{3,2,1,0:T(8,128)} %load_h.1, f32[3,8,8,512]{3,2,1,0:T(8,128)} %start_h.1, s32[8,8,512]{2,1,0:T(8,128)} %mask_h.1, bf16[24,24]{1,0:T(8,128)(2,1)} %stiff_h.1, bf16[48,128]{1,0:T(8,128)(2,1)} %constant.6.clone.tab0_h, ...), custom_call_target="tpu_custom_call" | custom-call | tf_op jit(solution)/shard_map/pallas_call | solution.py:640
  26.5 1.9 %add.3 = f32[3,8,8,512]{3,2,1,0:T(8,128)} add(f32[3,8,8,512]{3,2,1,0:T(8,128)} %get-tuple-element.7, f32[3,8,8,512]{3,2,1,0:T(8,128)} %get-tuple-element.8) | non-fusion elementwise | flops 98304 | bytes 1179648 | tf_op jit(solution)/shard_map/add | solution.py:681

commit v6 on v5

--- a/solution.py
+++ b/solution.py
@@ -314,6 +314,8 @@
             v = jnp.where(row8 % 4 == 3, 0.0, v)
             v = [v[:, b * quarter : (b + 1) * quarter] for b in range(4)]
             sc[p, k] = jnp.concatenate([jnp.where(low4, v[0], v[1]), jnp.where(low4, v[2], v[3])], axis=0).astype(BF16)
+
+    def pack_ends(p):
         sw[p, 2] = halves(xs[0]).astype(BF16)
         sw[p, 3] = halves(xs[B - 1]).astype(BF16)
 
@@ -327,8 +329,12 @@
     def begin(c):
         c.start()
 
-    def arrived(copy):
-        each(lambda k: copy(back(k)), lambda c: c.wait_recv())
+    def arrived(copy, ks=range(8)):
+        for k in ks:
+
+            @pl.when(exists(*NEAR[k]))
+            def _():
+                copy(back(k)).wait_recv()
 
     upd[...] = jnp.zeros_like(upd)
     vb[0] = jnp.zeros((48, nx), BF16)
@@ -338,6 +344,7 @@
         for d in range(3):
             xs[z, 8 * d : 8 * d + 8] = start[d, z]
     pack_field(0)
+    pack_ends(0)
     moves["tab0"].wait()
     moves["mask"].wait()
     mask_wide = jnp.concatenate([mask[z] for z in range(B)], axis=0).astype(F32)
@@ -443,6 +450,8 @@
         for side in range(2):
             scales = [se[16 * side + 8 * cz : 16 * side + 8 * cz + 8] for cz in range(2)]
             edge[side] = sums_of(wside[96 * side : 96 * side + 96], sides, scales)
+
+    def add_ends(p):
         for side in range(2):
             v = joined(rw[p, 2 + side].astype(F32))
             v = jnp.concatenate([v, shift_down(v)], axis=0).astype(BF16)
@@ -509,7 +518,9 @@
         for z in range(B):
             planes = vb[z : z + 3].reshape(144, nx)
             res[z] = stack(load, z) - apply(wmat[:, :144], planes, ss[z + 1], ss[z]) - three(idle[z]) * xs[z]
-        arrived(lambda k: field_copy(p, k))
+        arrived(lambda k: field_copy(p, k), range(6, 8))
+        add_ends(p)
+        arrived(lambda k: field_copy(p, k), range(6))
         add_edges(p)
         for z in range(B):
             sides = []
@@ -528,7 +539,9 @@
         @pl.when(p < 3)
         def _():
             pack_field(p + 1)
-            each(lambda k: field_copy(p + 1, k), begin)
+            each(lambda k: field_copy(p + 1, k), begin, range(6))
+            pack_ends(p + 1)
+            each(lambda k: field_copy(p + 1, k), begin, range(6, 8))
 
         @pl.when(p == 0)
         def _():

time: 28.6 us -> 29.3 us (1.024)
  Pallas kernels: 26.5 us -> 27.2 us
    pallas_call x1, Pallas kernels: 26.5 us -> 27.2 us  [body(): pl.pallas_call(functools.partial(kernel, where, n_z, n_y), out_shape=[jax...]
where the time goes in v6:
time: 29.3 us; the launch traced here: 29.1 us
  Pallas kernels  27.2 us (93%)
  other arithmetic  1.92 us (7%)
    pallas_call x1, Pallas kernels, body(): pl.pallas_call(functools.partial(kernel, where, n_z, n_y), out_shape=[jax...  27.2 us
    add x1, other arithmetic, body(): return smooth + fix  1.92 us

profile of v6, /device:TPU:3, one launch (start us, length us, event | category | flops | bytes accessed | tf_op | source)
XLA Modules:
  0.0 29.1 jit_solution(11103682076270896663)
XLA Ops:
  0.0 27.2 %shard_map.73 = (f32[3,8,8,512]{3,2,1,0:T(8,128)}, f32[3,8,8,512]{3,2,1,0:T(8,128)}) custom-call(f32[3,8,8,512]{3,2,1,0:T(8,128)} %load_h.1, f32[3,8,8,512]{3,2,1,0:T(8,128)} %start_h.1, s32[8,8,512]{2,1,0:T(8,128)} %mask_h.1, bf16[24,24]{1,0:T(8,128)(2,1)} %stiff_h.1, bf16[48,128]{1,0:T(8,128)(2,1)} %constant.6.clone.tab0_h, ...), custom_call_target="tpu_custom_call" | custom-call | tf_op jit(solution)/shard_map/pallas_call | solution.py:653
  27.2 1.9 %add.3 = f32[3,8,8,512]{3,2,1,0:T(8,128)} add(f32[3,8,8,512]{3,2,1,0:T(8,128)} %get-tuple-element.7, f32[3,8,8,512]{3,2,1,0:T(8,128)} %get-tuple-element.8) | non-fusion elementwise | flops 98304 | bytes 1179648 | tf_op jit(solution)/shard_map/add | solution.py:694
